TPU v7x, 32 devices: a whole 2x2x4 slice. The times are simulated.
32 devices in a mesh: expert: 8 (over y, x, core), context: 4 (over z).
Axes of the slice: x: 2, y: 2, z: 4, core: 2. Of those that a mesh axis runs over, the one named last changes fastest.
Arguments:
- tokens: bfloat16 [8192, 768], P(('expert', 'context')), may hold values from -6 to 6
- gain_attn: float32 [768], replicated, may hold values from 0.5 to 1.5
- w_query: bfloat16 [768, 768], replicated, may hold values from -0.21875 to 0.21875
- w_key: bfloat16 [768, 768], replicated, may hold values from -0.21875 to 0.21875
- w_value: bfloat16 [768, 768], replicated, may hold values from -0.21875 to 0.21875
- w_proj: bfloat16 [768, 768], replicated, may hold values from -3 to 3
- bias_table: float32 [32, 12], replicated, may hold values from -4 to 4
- gain_moe: float32 [768], replicated, may hold values from 0.5 to 1.5
- w_router: bfloat16 [768, 8], replicated, may hold values from -0.15625 to 0.15625
- w_up: bfloat16 [8, 768, 3072], P('expert'), may hold values from -0.21875 to 0.21875
- w_down: bfloat16 [8, 3072, 768], P('expert'), may hold values from -0.109375 to 0.109375
- routes: int32 [8192, 2], P(('expert', 'context')), may hold values from 0 to 7, all different within a row; in each aligned block of 256 rows (0 to 255, 256 to 511, ...) at most 128 rows name the same one
- bucket_ids: int32 [1024], replicated, may hold values from 0 to 31, as said below
- cotangent: bfloat16 [8192, 768], P(('expert', 'context')), may hold values from -6 to 6
Outputs:
- output: bfloat16 [8192, 768], P(('expert', 'context'))
- grad_tokens: bfloat16 [8192, 768], P(('expert', 'context'))
- grad_gain_attn: float32 [768], replicated
- grad_query: float32 [768, 768], replicated
- grad_key: float32 [768, 768], replicated
- grad_value: float32 [768, 768], replicated
- grad_proj: float32 [768, 768], replicated
- grad_table: float32 [32, 12], replicated
- grad_gain_moe: float32 [768], replicated
- grad_router: float32 [768, 8], replicated
- grad_up: float32 [8, 768, 3072], P('expert', None, 'context')
- grad_down: float32 [8, 3072, 768], P('expert', 'context')
Inputs may be any that keep to these rules, and one draw needn't show every extreme that they name: `routes`: in each aligned block of 256 rows (the rows of one device) no expert is named by more than 128 rows, a bound that some block reaches; the 2 experts of a row differ. `bucket_ids`: entry d is the bucket of a key d positions before its query; the entries never fall, rise by at most one from one distance to the next, entry 0 is 0 and the last entry is 31.
All inputs are finite; a program needn't handle non-finite values.
Results may differ from a plain program's by a relative error of at most 0.02.
Values may be sent and summed in bfloat16 or wider, within the bound.
No kernel may reach another device: no remote copies, remote signals or barrier semaphores. Data moves between devices by JAX's collectives and lax.ppermute only.
A program may use at most 192 MiB of HBM per device.

v0:
```python
from functools import partial

import jax
import jax.numpy as jnp
from jax import lax
from jax.experimental import pallas as pl
from jax.experimental.pallas import tpu as pltpu
from jax.sharding import PartitionSpec as P

HEADS = 12
EPSILON = 1e-06
HIGHEST = lax.Precision.HIGHEST
MASKED = -1000000000.0
F32 = jnp.float32
BF16 = jnp.bfloat16
VMEM_LIMIT = 56 * 1024 * 1024
FF_TILE = 512
SPARE = 8
ROW_TILE = 512


def dot(left, right, dims=((1,), (0,))):
    return lax.dot_general(left, right, (dims, ((), ())), preferred_element_type=F32)


def normalize(value, gain):
    scale = lax.rsqrt(jnp.mean(value * value, axis=1, keepdims=True) + EPSILON)
    return (value * scale * gain, scale)


def normalize_back(grad, value, scale, gain):
    normal = value * scale
    inner = grad * gain
    gain_grad = jnp.sum(grad * normal, axis=0)
    value_grad = scale * (inner - normal * jnp.mean(inner * normal, axis=1, keepdims=True))
    return (value_grad, gain_grad)


def shift(value, axis, step):
    count = lax.axis_size(axis)
    return lax.ppermute(value, axis, [(i, (i + step) % count) for i in range(count)])


def swap(value, axis, bit):
    count = lax.axis_size(axis)
    return lax.ppermute(value, axis, [(i, i ^ bit) for i in range(count)])


def after(value, *others):
    return lax.optimization_barrier((value, others))[0]


def ring_parts(value, axis, hold=None):
    count = lax.axis_size(axis)
    parts = [(0, value)]
    right = left = value
    for step in range(1, count // 2 + 1):
        if step == 2 and hold is not None:
            right, left = after((right, left), hold)
        right = shift(right, axis, 1)
        parts.append((step, right))
        if step <= (count - 1) // 2:
            left = shift(left, axis, -1)
            parts.append((count - step, left))
    return parts


def in_order(parts, axis):
    count = lax.axis_size(axis)
    here = lax.axis_index(axis)
    value = parts[0][1]
    size = value.shape[0]
    whole = jnp.zeros((count * size,) + value.shape[1:], value.dtype)
    for step, part in parts:
        whole = lax.dynamic_update_slice_in_dim(
            whole, part, lax.rem(here - step + count, count) * size, 0
        )
    return whole


def bit_orders(count):
    bits = [1 << i for i in range(count.bit_length() - 1)]
    return bits[:1] + bits[:0:-1]


def halve_sum(value, axis, bits, low=BF16):
    here = lax.axis_index(axis)
    for bit in bits:
        pair = value.reshape((2, value.shape[0] // 2) + value.shape[1:])
        mine = lax.rem(here // bit, 2)
        kept = lax.dynamic_index_in_dim(pair, mine, 0, keepdims=False)
        sent = lax.dynamic_index_in_dim(pair, 1 - mine, 0, keepdims=False).astype(low)
        value = kept.astype(F32) + swap(sent, axis, bit).astype(F32)
    return value[0]


def double_gather(value, axis, order):
    for bit in order:
        value = jnp.stack([value, swap(value, axis, bit)])
    return value


def attend_kernel(tokens, gain, weight, bias, normed, qkv, mixed, exact, log_total, tiles):
    length = tokens.shape[0]
    count, size, tile = mixed.shape

    @pl.when(pl.program_id(0) == 0)
    def _():
        def body(i, carry):
            part = pl.ds(i * tile, tile)
            normal, unused = normalize(tokens[part, :].astype(F32), gain[...])
            normed[part, :] = normal.astype(BF16)
            return carry

        lax.fori_loop(0, count, body, 0)

    weight_all = weight[...].reshape(3 * size, weight.shape[2])
    key_parts = []
    for i in range(count):
        part = dot(weight_all, normed[i * tile : (i + 1) * tile, :], ((1,), (1,)))
        low = part.astype(BF16)
        for j in range(3):
            qkv[j, :, i * tile : (i + 1) * tile] = low[j * size : (j + 1) * size, :]
        key_parts.append(part[size : 2 * size, :].T.astype(BF16))
        wide = jnp.broadcast_to(bias[0, :, i * tile : (i + 2) * tile], (tile, 2 * tile))
        turned = pltpu.roll(wide, tile, 1, stride=1, stride_axis=0)
        tiles[(count - 1 - i) * tile : (count - i) * tile, :] = turned[:, :tile]
    keys = jnp.concatenate(key_parts, axis=0)
    factor = size ** (-0.5)
    for i in range(count):
        cols = slice(i * tile, (i + 1) * tile)
        many = (i + 1) * tile
        scores = dot(keys[:many], qkv[0, :, cols]) * factor + tiles[length - many :, :]
        peak = jnp.max(scores, axis=0, keepdims=True)
        weights = jnp.exp(scores - peak)
        total = jnp.sum(weights, axis=0, keepdims=True)
        result = dot(qkv[2, :, :many], weights.astype(BF16)) * (1.0 / total)
        exact[0, :, cols] = result
        mixed[i, :, :] = result.astype(BF16)
        log_total[0, :, cols] = peak + jnp.log(total)


def fold(grid):
    tile = grid.shape[0]
    value = jnp.concatenate([jnp.zeros_like(grid), grid], axis=1)
    half = tile // 2
    while half >= 8:
        value = value[:half] + pltpu.roll(value[half:], 2 * tile - half, 1)
        half //= 2
    return value


def attend_back_kernel(
    qkv, normed, bias, log_total, exact, grads_in, grads, weight_grads, diagonals,
    tiles, sums, keys_acc, values_acc, query_acc,
):
    count, size, tile = grads_in.shape
    factor = size ** (-0.5)
    queries, values, outs, deltas = [], [], [], []
    keys = []
    for i in range(count):
        cols = slice(i * tile, (i + 1) * tile)
        queries.append(qkv[0, :, cols].astype(F32).T.astype(BF16))
        keys.append(qkv[1, :, cols].astype(F32).T.astype(BF16))
        values.append(qkv[2, :, cols].astype(F32).T.astype(BF16))
        out = grads_in[i].astype(F32)
        outs.append(out.T.astype(BF16))
        deltas.append(jnp.sum(out * exact[0, :, cols], axis=0, keepdims=True))
        wide = jnp.broadcast_to(bias[0, :, i * tile : (i + 2) * tile], (tile, 2 * tile))
        turned = pltpu.roll(wide, tile, 1, stride=1, stride_axis=0)
        tiles[i] = turned[:, :tile]
    for d in range(count):
        for j in range(count - d):
            i = j + d
            cols = slice(i * tile, (i + 1) * tile)
            scores = dot(keys[j], qkv[0, :, cols]) * factor + tiles[d]
            probs = jnp.exp(scores - log_total[0, :, cols])
            prob_grads = dot(values[j], grads_in[i])
            score_grads = probs * (prob_grads - deltas[i])
            low = score_grads.astype(BF16)
            value_part = dot(probs.astype(BF16), outs[i])
            key_part = dot(low, queries[i])
            query_part = dot(qkv[1, :, j * tile : (j + 1) * tile], low)
            if j == 0:
                sums[...] = score_grads
            else:
                sums[...] += score_grads
            if d == 0:
                values_acc[j] = value_part
                keys_acc[j] = key_part
                query_acc[i] = query_part
            else:
                values_acc[j] += value_part
                keys_acc[j] += key_part
                query_acc[i] += query_part
        rows = fold(sums[...])
        line = rows[0:1]
        for r in range(1, 8):
            line = line + pltpu.roll(rows[r : r + 1], 2 * tile - r, 1)
        if d == 0:
            diagonals[0, :, : 2 * tile] = line
        else:
            diagonals[0, :, d * tile : (d + 1) * tile] += line[:, :tile]
            diagonals[0, :, (d + 1) * tile : (d + 2) * tile] = line[:, tile:]
    total = None
    for i in range(count):
        query_part = (query_acc[i] * factor).astype(BF16)
        key_part = (keys_acc[i] * factor).T.astype(BF16)
        value_part = values_acc[i].T.astype(BF16)
        grads[i, 0] = query_part
        grads[i, 1] = key_part
        grads[i, 2] = value_part
        stacked = jnp.concatenate([query_part, key_part, value_part], axis=0)
        part = dot(stacked, normed[i * tile : (i + 1) * tile, :])
        total = part if total is None else total + part
    for j in range(3):
        weight_grads[j] = total[j * size : (j + 1) * size, :].astype(BF16)


def gelu_parts(hidden):
    below = 0.5 * (1.0 + lax.erf(hidden * (0.5**0.5)))
    density = jnp.exp(-0.5 * hidden * hidden) * 0.3989422804014327
    return (hidden * below).astype(BF16), below + hidden * density


def scaled_rows(target, start, gate, upstream):
    lanes, capacity = gate.shape[0], gate.shape[2]
    for i in range(lanes):
        column = jnp.broadcast_to(gate[i], (8, capacity)).T[:, :1]
        grads = column * upstream[i, :capacity, :].astype(F32)
        target[start + i * capacity : start + (i + 1) * capacity, :] = grads.astype(BF16)


def expert_kernel(rows_in, upstream, gate, up, down, outs, row_grads, out_grads, acc, sums, out_acc):
    step = pl.program_id(0)
    lanes, capacity = gate.shape[0], gate.shape[2]

    @pl.when(step == 0)
    def _():
        scaled_rows(out_grads, 0, gate, upstream)
        acc[...] = jnp.zeros_like(acc)
        out_acc[...] = jnp.zeros_like(out_acc)
        sums[...] = jnp.zeros_like(sums)

    hidden = dot(rows_in[...], up[...])
    active_grads = dot(out_grads[...], down[...], ((1,), (1,)))
    low_active, slope = gelu_parts(hidden)
    low_grads = (active_grads * slope).astype(BF16)
    out_acc[...] += dot(low_active, down[...])
    acc[...] += dot(low_grads, up[...], ((1,), (1,)))
    weighted = low_active.astype(F32) * active_grads
    part = weighted[:, :128]
    for i in range(1, weighted.shape[1] // 128):
        part = part + weighted[:, i * 128 : (i + 1) * 128]
    sums[...] += part

    @pl.when(step == pl.num_programs(0) - 1)
    def _():
        outs[...] = out_acc[...].astype(BF16)
        low = acc[...].astype(BF16)
        for i in range(lanes):
            rows = slice(i * capacity, (i + 1) * capacity)
            row_grads[i, :capacity, :] = low[rows, :]
            line = jnp.sum(sums[rows, :].T, axis=0, keepdims=True)
            high = line.astype(BF16).astype(F32)
            both = jnp.concatenate([high, line - high, jnp.zeros((SPARE - 2, capacity), F32)])
            row_grads[i, capacity:, :] = jnp.zeros((SPARE, row_grads.shape[2]), BF16)
            row_grads[i, capacity:, :capacity] = both.astype(BF16)


def expert_grads_kernel(
    index, own_rows, other_rows, own_upstream, other_upstream, own_gate, other_gate, up, down,
    up_grad, down_grad, turned, out_grads, active, hidden_grads,
):
    half = own_rows.shape[0]
    tile = min(ROW_TILE, half)

    @pl.when(pl.program_id(0) == 0)
    def _():
        scaled_rows(out_grads, 0, own_gate, own_upstream)
        scaled_rows(out_grads, half, other_gate, other_upstream)
        for start in range(0, half, tile):
            rows = slice(start, start + tile)
            turned[:, rows] = own_rows[rows, :].T
            turned[:, half + start : half + start + tile] = other_rows[rows, :].T

    for base, source in ((0, own_rows), (half, other_rows)):
        for start in range(0, half, tile):
            rows = slice(base + start, base + start + tile)
            hidden = dot(source[start : start + tile, :], up[...])
            active_grads = dot(out_grads[rows, :], down[...], ((1,), (1,)))
            low_active, slope = gelu_parts(hidden)
            active[rows, :] = low_active
            hidden_grads[rows, :] = (active_grads * slope).astype(BF16)
    up_grad[0] = dot(turned[...], hidden_grads[...]).astype(BF16)
    down_grad[0] = dot(active[...], out_grads[...], ((0,), (0,))).astype(BF16)


def params():
    return pltpu.CompilerParams(
        dimension_semantics=("arbitrary",), vmem_limit_bytes=VMEM_LIMIT
    )


def cost(flops, size):
    return pl.CostEstimate(flops=flops, bytes_accessed=size, transcendentals=0)


def attend(tokens, gain, weight, bias, count):
    length, width = tokens.shape
    group = bias.shape[0]
    size = weight.shape[1] // group
    tile = length // count
    return pl.pallas_call(
        attend_kernel,
        grid=(group,),
        in_specs=[
            pl.BlockSpec((length, width), lambda h: (0, 0)),
            pl.BlockSpec((1, width), lambda h: (0, 0)),
            pl.BlockSpec((3, size, width), lambda h: (0, h, 0)),
            pl.BlockSpec((1, 1, length + tile), lambda h: (h, 0, 0)),
        ],
        out_specs=[
            pl.BlockSpec((length, width), lambda h: (0, 0)),
            pl.BlockSpec((3, size, length), lambda h: (0, h, 0)),
            pl.BlockSpec((count, size, tile), lambda h: (0, h, 0)),
            pl.BlockSpec((1, size, length), lambda h: (h, 0, 0)),
            pl.BlockSpec((1, 1, length), lambda h: (h, 0, 0)),
        ],
        out_shape=[
            jax.ShapeDtypeStruct((length, width), BF16),
            jax.ShapeDtypeStruct((3, group * size, length), BF16),
            jax.ShapeDtypeStruct((count, group * size, tile), BF16),
            jax.ShapeDtypeStruct((group, size, length), F32),
            jax.ShapeDtypeStruct((group, 1, length), F32),
        ],
        scratch_shapes=[pltpu.VMEM((length, tile), F32)],
        compiler_params=params(),
        cost_estimate=cost(14 * length * width * size * group, 8 * length * width),
        name="attend",
    )(tokens, gain, weight, bias)


def attend_back(qkv, normed, bias, log_total, exact, grads_in):
    length, width = normed.shape
    count, _, tile = grads_in.shape
    group, size, _ = exact.shape
    return pl.pallas_call(
        attend_back_kernel,
        grid=(group,),
        in_specs=[
            pl.BlockSpec((3, size, length), lambda h: (0, h, 0)),
            pl.BlockSpec((length, width), lambda h: (0, 0)),
            pl.BlockSpec((1, 1, length + tile), lambda h: (h, 0, 0)),
            pl.BlockSpec((1, 1, length), lambda h: (h, 0, 0)),
            pl.BlockSpec((1, size, length), lambda h: (h, 0, 0)),
            pl.BlockSpec((count, size, tile), lambda h: (0, h, 0)),
        ],
        out_specs=[
            pl.BlockSpec((count, 3, size, tile), lambda h: (0, 0, h, 0)),
            pl.BlockSpec((3, size, width), lambda h: (0, h, 0)),
            pl.BlockSpec((1, 1, length + tile), lambda h: (h, 0, 0)),
        ],
        out_shape=[
            jax.ShapeDtypeStruct((count, 3, group * size, tile), BF16),
            jax.ShapeDtypeStruct((3, group * size, width), BF16),
            jax.ShapeDtypeStruct((group, 1, length + tile), F32),
        ],
        scratch_shapes=[
            pltpu.VMEM((count, tile, tile), F32),
            pltpu.VMEM((tile, tile), F32),
            pltpu.VMEM((count, tile, size), F32),
            pltpu.VMEM((count, tile, size), F32),
            pltpu.VMEM((count, size, tile), F32),
        ],
        compiler_params=params(),
        cost_estimate=cost(18 * length * width * size * group, 8 * length * width),
        name="attend_back",
    )(qkv, normed, bias, log_total, exact, grads_in)


def expert(rows_in, upstream, gate, up, down):
    rows, width = rows_in.shape
    hidden = up.shape[1]
    lanes, _, capacity = gate.shape
    return pl.pallas_call(
        expert_kernel,
        grid=(hidden // FF_TILE,),
        in_specs=[
            pl.BlockSpec((rows, width), lambda f: (0, 0)),
            pl.BlockSpec(upstream.shape, lambda f: (0, 0, 0)),
            pl.BlockSpec(gate.shape, lambda f: (0, 0, 0)),
            pl.BlockSpec((width, FF_TILE), lambda f: (0, f)),
            pl.BlockSpec((FF_TILE, width), lambda f: (f, 0)),
        ],
        out_specs=[
            pl.BlockSpec((rows, width), lambda f: (0, 0)),
            pl.BlockSpec((lanes, capacity + SPARE, width), lambda f: (0, 0, 0)),
        ],
        out_shape=[
            jax.ShapeDtypeStruct((rows, width), BF16),
            jax.ShapeDtypeStruct((lanes, capacity + SPARE, width), BF16),
        ],
        scratch_shapes=[
            pltpu.VMEM((rows, width), BF16),
            pltpu.VMEM((rows, width), F32),
            pltpu.VMEM((rows, 128), F32),
            pltpu.VMEM((rows, width), F32),
        ],
        compiler_params=params(),
        cost_estimate=cost(10 * rows * width * hidden, 4 * width * hidden),
        name="expert",
    )(rows_in, upstream, gate, up, down)


def expert_grads(index, own_rows, other_rows, own_upstream, other_upstream, own_gate, other_gate, up, down, count, steps):
    half, width = own_rows.shape
    hidden = up.shape[1]
    share = hidden // count
    whole = pl.BlockSpec((half, width), lambda s, i: (0, 0))
    slots = pl.BlockSpec(own_upstream.shape, lambda s, i: (0, 0, 0))
    gates = pl.BlockSpec(own_gate.shape, lambda s, i: (0, 0, 0))
    return pl.pallas_call(
        expert_grads_kernel,
        grid_spec=pltpu.PrefetchScalarGridSpec(
            num_scalar_prefetch=1,
            grid=(steps,),
            in_specs=[
                whole,
                whole,
                slots,
                slots,
                gates,
                gates,
                pl.BlockSpec((width, share), lambda s, i: (0, i[0] + s)),
                pl.BlockSpec((share, width), lambda s, i: (i[0] + s, 0)),
            ],
            out_specs=[
                pl.BlockSpec((1, width, share), lambda s, i: (s, 0, 0)),
                pl.BlockSpec((1, share, width), lambda s, i: (s, 0, 0)),
            ],
            scratch_shapes=[
                pltpu.VMEM((width, 2 * half), BF16),
                pltpu.VMEM((2 * half, width), BF16),
                pltpu.VMEM((2 * half, share), BF16),
                pltpu.VMEM((2 * half, share), BF16),
            ],
        ),
        out_shape=[
            jax.ShapeDtypeStruct((steps, width, share), BF16),
            jax.ShapeDtypeStruct((steps, share, width), BF16),
        ],
        compiler_params=params(),
        cost_estimate=cost(16 * half * width * share * steps, 8 * half * width),
        name="expert_grads",
    )(index, own_rows, other_rows, own_upstream, other_upstream, own_gate, other_gate, up, down)


def assemble_kernel(
    bits, chunk, index, near, far, query, key, value,
    query_grad, key_grad, value_grad, proj_grad, small_sum, gain_sum,
):
    outer = bits[1:]
    lanes = 1 << len(bits)
    count, depth, half = near.shape[-3:]
    own = index[0]
    first = pl.program_id(0) == 0

    def block(lane, z):
        turn = own ^ lane
        steps = [lax.rem(turn // bit, 2) for bit in outer]
        places = [jnp.where(first, a, b) for a, b in zip(steps, steps[::-1])]
        side = lax.rem(turn // bits[0], 2) == 0
        at = (0, *places, z)
        return jnp.where(side, near[at], far[at]).astype(F32)

    order = []
    for i in range(lanes):
        lane = 0
        for j, bit in enumerate(bits):
            lane += bit * ((i >> (len(bits) - 1 - j)) & 1)
        order.append(lane)
    blocks = [[block(lane, z) for z in range(count)] for lane in order]
    part = chunk // 3
    share = depth - chunk - SPARE
    for i in range(lanes):
        total = blocks[i][0][chunk : chunk + SPARE]
        for z in range(1, count):
            total = total + blocks[i][z][chunk : chunk + SPARE]
        small_sum[i * SPARE : (i + 1) * SPARE, :] = total
    proj_grad[...] = jnp.concatenate(
        [blocks[i][z][chunk + SPARE :] for i in range(lanes) for z in range(count)], axis=0
    )
    total = None
    for j, (weight, grad) in enumerate(
        ((query, query_grad), (key, key_grad), (value, value_grad))
    ):
        rows = [
            blocks[i][z][j * part : (j + 1) * part] for z in range(count) for i in range(lanes)
        ]
        whole = jnp.concatenate(rows, axis=0)[: grad.shape[1]].T
        grad[...] = whole
        sums = jnp.sum(whole * weight[...].astype(F32), axis=1, keepdims=True)
        total = sums if total is None else total + sums
    gain_sum[...] = total


def assemble(index, near, far, query, key, value, bits, chunk):
    shape = near.shape
    half = shape[-1]
    width = query.shape[0]
    lanes = 1 << len(bits)
    rows = pl.BlockSpec((half, width), lambda s, i: (s, 0))
    cols = pl.BlockSpec((width, half), lambda s, i: (0, s))
    pack = pl.BlockSpec((1,) + shape[1:], lambda s, i: (s,) + (0,) * (len(shape) - 1))
    return pl.pallas_call(
        partial(assemble_kernel, bits, chunk),
        grid_spec=pltpu.PrefetchScalarGridSpec(
            num_scalar_prefetch=1,
            grid=(shape[0],),
            in_specs=[pack, pack, rows, rows, rows],
            out_specs=[
                rows,
                rows,
                rows,
                cols,
                pl.BlockSpec((lanes * SPARE, half), lambda s, i: (0, s)),
                pl.BlockSpec((half, 1), lambda s, i: (s, 0)),
            ],
        ),
        out_shape=[jax.ShapeDtypeStruct((width, width), F32)] * 4
        + [
            jax.ShapeDtypeStruct((lanes * SPARE, width), F32),
            jax.ShapeDtypeStruct((width, 1), F32),
        ],
        compiler_params=params(),
        name="assemble",
    )(index, near, far, query, key, value)


def token_back_kernel(
    returns, dispatch, gates, chosen, middle, cotangent, gain, routed, router, proj,
    middle_grads, branch_grads, mixed_grads, gain_grad, router_grad,
):
    experts, depth, width = returns.shape
    capacity = depth - SPARE
    grads = None
    columns = []
    for i in range(experts):
        select = dispatch[:, i * capacity : (i + 1) * capacity]
        part = dot(select, returns[i, :capacity, :])
        grads = part if grads is None else grads + part
        lines = returns[i, capacity:, :].astype(F32)
        line = (lines[0:1] + lines[1:2])[:, :capacity]
        columns.append(jnp.sum(select.astype(F32) * line, axis=1, keepdims=True))
    total = columns[0]
    for column in columns[1:]:
        total = total + column
    logit_grads = []
    for i in range(experts):
        grad = (columns[i] - gates[:, i : i + 1] * total) * chosen[:, i : i + 1]
        logit_grads.append(grad)
        grads = grads + grad * router[i : i + 1, :]
        router_grad[i : i + 1, :] = jnp.sum(grad * routed[...].astype(F32), axis=0, keepdims=True)
    value = middle[...]
    scale = lax.rsqrt(jnp.mean(value * value, axis=1, keepdims=True) + EPSILON)
    normal = value * scale
    gain_grad[...] = jnp.sum(grads * normal, axis=0, keepdims=True)
    inner = grads * gain[...]
    back = scale * (inner - normal * jnp.mean(inner * normal, axis=1, keepdims=True))
    result = cotangent[...].astype(F32) + back
    middle_grads[...] = result
    low = result.astype(BF16)
    branch_grads[...] = low
    mixed_grads[...] = dot(proj[...], low, ((1,), (1,))).astype(BF16)


def token_back(returns, dispatch, gates, chosen, middle, cotangent, gain, routed, router, proj):
    rows, width = middle.shape
    return pl.pallas_call(
        token_back_kernel,
        out_shape=[
            jax.ShapeDtypeStruct((rows, width), F32),
            jax.ShapeDtypeStruct((rows, width), BF16),
            jax.ShapeDtypeStruct((width, rows), BF16),
            jax.ShapeDtypeStruct((1, width), F32),
            jax.ShapeDtypeStruct(router.shape, F32),
        ],
        compiler_params=pltpu.CompilerParams(vmem_limit_bytes=VMEM_LIMIT),
        name="token_back",
    )(returns, dispatch, gates, chosen, middle, cotangent, gain, routed, router, proj)


def chosen_softmax(logits, chosen, axis):
    peak = jnp.max(jnp.where(chosen, logits, -jnp.inf), axis=axis, keepdims=True)
    peak = jnp.where(peak > -jnp.inf, peak, 0.0)
    parts = jnp.where(chosen, jnp.exp(jnp.where(chosen, logits, peak) - peak), 0.0)
    total = jnp.sum(parts, axis=axis, keepdims=True)
    return parts / jnp.where(total > 0.0, total, 1.0)


def to_experts(value):
    return exchange(value, "expert")


def to_context(value):
    return exchange(value, "context")


def exchange(value, axis):
    return lax.all_to_all(value, axis, split_axis=0, concat_axis=0)


def exchange_steps(value, axis, send):
    count = lax.axis_size(axis)
    here = lax.axis_index(axis)
    whole = jnp.zeros_like(value)
    for step in sorted(range(count), key=lambda k: (k != 0, -min(k, count - k))):
        target, source, part = send(here, step)
        piece = lax.dynamic_slice_in_dim(value, target, 1, 0)
        whole = lax.dynamic_update_slice_in_dim(whole, part(piece) if step else piece, source, 0)
    return whole


def expert_steps(value):
    def send(here, step):
        return here ^ step, here ^ step, lambda piece: swap(piece, "expert", step)

    return exchange_steps(value, "expert", send)


def context_steps(value, arrivals=None):
    count = lax.axis_size("context")

    def send(here, step):
        target, source = lax.rem(here + step, count), lax.rem(here - step + count, count)

        def part(piece):
            piece = shift(piece, "context", step)
            if arrivals is not None:
                arrivals.append(piece)
            return piece

        return target, source, part

    return exchange_steps(value, "context", send)


def shards(
    tokens,
    gain_attn,
    w_query,
    w_key,
    w_value,
    w_proj,
    bias_table,
    gain_moe,
    w_router,
    w_up,
    w_down,
    routes,
    bucket_ids,
    cotangent,
):
    rows, width = tokens.shape
    size = width // HEADS
    experts = w_router.shape[1]
    buckets = bias_table.shape[0]
    picks = routes.shape[1]
    capacity = 2 * rows * picks // experts
    slots = experts * capacity
    count = lax.axis_size("context")
    lanes = lax.axis_size("expert")
    here = lax.axis_index("context")
    own = lax.axis_index("expert")
    length = rows * count
    group = -(-HEADS // count)
    held = group * size
    extra = count * group - HEADS

    token_parts = ring_parts(tokens, "context")

    expert_ids = jnp.arange(experts, dtype=jnp.int32)
    order = jnp.arange(rows, dtype=jnp.int32)
    earlier = (order[:, None] > order[None, :]).astype(BF16)

    def routing(block):
        chosen = jnp.any(block[:, :, None] == expert_ids[None, None, :], axis=1)
        member = chosen.astype(BF16)
        place = dot(earlier, member).astype(jnp.int32)
        dispatch = (
            (place[:, :, None] == jnp.arange(capacity, dtype=jnp.int32)[None, None, :])
            & chosen[:, :, None]
        ).astype(BF16)
        return chosen, member, dispatch.reshape(rows, slots)

    chosen, member, dispatch = routing(routes)

    def slots_of(dispatch, block):
        sent = dot(dispatch, block, ((0,), (0,))).astype(BF16)
        return sent.reshape(experts, capacity, width)

    def upstream_sent(member, dispatch, block):
        choices = dot(member, dispatch, ((0,), (0,))).astype(BF16)
        choices = jnp.transpose(choices.reshape(experts, experts, capacity), (1, 0, 2))
        choices = jnp.pad(choices, ((0, 0), (0, 0), (0, width - capacity)))
        return jnp.concatenate([slots_of(dispatch, block), choices], axis=1)

    partner = count // 2

    def head_rows(weight):
        whole = jnp.pad(weight, ((0, 0), (0, extra * size)))
        return lax.dynamic_slice_in_dim(whole, here * held, held, 1).T

    head_weights = jnp.stack([head_rows(w) for w in (w_query, w_key, w_value)])

    own_sent, head_weights = after(
        (upstream_sent(member, dispatch, cotangent), head_weights), token_parts[2][1]
    )
    upstream_slots = to_experts(own_sent)
    sequence = in_order(token_parts, "context")
    cotangent_other, routes_other = after((cotangent, routes.T), sequence)
    cotangent_other = swap(cotangent_other, "context", partner)
    routes_other = swap(routes_other, "context", partner)

    bucket_match = (
        bucket_ids[:, None] == jnp.arange(buckets, dtype=jnp.int32)[None, :]
    ).astype(F32)
    per_distance = lax.dot_general(
        jnp.pad(bias_table, ((0, 0), (0, extra))), bucket_match, (((0,), (1,)), ((), ())),
        precision=HIGHEST,
    )
    bias = jnp.pad(
        lax.dynamic_slice_in_dim(per_distance, here * group, group, 0),
        ((0, 0), (rows, 0)),
        constant_values=MASKED,
    )[:, None, :]
    normed, qkv, mixed_parts, exact, log_total = attend(
        sequence, gain_attn[None, :], head_weights, bias, count
    )
    mixed_parts, upstream_slots, cotangent_other, routes_other = lax.optimization_barrier(
        (mixed_parts, upstream_slots, cotangent_other, routes_other)
    )
    unused, member_other, dispatch_other = routing(routes_other.T)
    upstream_other = to_experts(upstream_sent(member_other, dispatch_other, cotangent_other))
    mixed = context_steps(mixed_parts).reshape(count * held, rows)[:width]
    source = tokens.astype(F32)
    middle = source + dot(mixed, w_proj, ((0,), (0,)))
    moe_normal, moe_scale = normalize(middle, gain_moe)
    routed = moe_normal.astype(BF16)

    logits = dot(routed, w_router)
    gates = chosen_softmax(logits, chosen, 1)

    def gates_of(received, upstream):
        choices = jnp.moveaxis(upstream[:, capacity:, :capacity], 1, 0) > 0.5
        slot_logits = dot(w_router, received, ((0,), (1,))).reshape(experts, lanes, capacity)
        slot_gates = chosen_softmax(slot_logits, choices, 0)
        return lax.dynamic_index_in_dim(slot_gates, own, 0, keepdims=False)[:, None, :]

    sent, upstream_other = lax.optimization_barrier((slots_of(dispatch, routed), upstream_other))
    received = to_experts(sent).reshape(slots, width)
    routed_other = swap(routed, "context", partner)
    received, routed_other = lax.optimization_barrier((received, routed_other))
    received_other = to_experts(slots_of(dispatch_other, routed_other)).reshape(slots, width)
    slot_gate = gates_of(received, upstream_slots)
    expert_out, row_grads = expert(received, upstream_slots, slot_gate, w_up[0], w_down[0])
    row_grads, received_other = lax.optimization_barrier((row_grads, received_other))
    row_returns = to_experts(row_grads)

    quarter = partner // 2
    mine = lax.rem(here // quarter, 2)
    first = (here // partner) * partner
    other_gate = gates_of(received_other, upstream_other)

    def gradients(start, hold):
        return expert_grads(
            after(start, hold)[None],
            received,
            received_other,
            upstream_slots,
            upstream_other,
            slot_gate,
            other_gate,
            w_up[0],
            w_down[0],
            count,
            quarter,
        )

    up_sent, down_sent = gradients(first + (1 - mine) * quarter, row_grads)
    up_kept, down_kept = gradients(first + mine * quarter, down_sent)
    row_returns, down_sent, up_kept, down_kept = lax.optimization_barrier(
        (row_returns, down_sent, up_kept, down_kept)
    )
    up_arrived = swap(up_sent, "context", quarter)
    low_bits = [1 << i for i in range(quarter.bit_length() - 1)][::-1]
    spread = dispatch.reshape(rows, experts, capacity).astype(F32)
    middle_grads, branch_grads, mixed_grads, gain_moe_grad, router_grad = token_back(
        row_returns,
        dispatch,
        gates,
        chosen.astype(F32),
        middle,
        cotangent,
        gain_moe[None, :],
        routed,
        w_router.astype(F32).T,
        w_proj,
    )
    arrivals = []
    grads_in = context_steps(
        jnp.pad(mixed_grads, ((0, extra * size), (0, 0))).reshape(count, held, rows),
        arrivals,
    )
    bits = bit_orders(lanes)
    out_returns = to_experts(after(expert_out, arrivals[0]).reshape(experts, capacity, width))
    grads_in, up_arrived = lax.optimization_barrier((grads_in, up_arrived))
    proj_part = dot(mixed, branch_grads).astype(BF16).reshape(lanes, width // lanes, width)
    proj_part = halve_sum(proj_part, "expert", bits).astype(BF16)
    proj_part = context_steps(proj_part.reshape(count, width // (lanes * count), width))
    proj_rows = jnp.sum(proj_part.astype(F32), axis=0).astype(BF16)

    grads_out, weight_grads, diagonals = attend_back(
        qkv, normed, bias, log_total, exact, grads_in
    )
    weight_grads, out_returns = lax.optimization_barrier((weight_grads, out_returns))
    cut = down_sent.shape[1] // 2
    down_first = swap(after(down_sent[:, :cut], up_arrived), "context", quarter)
    weight_grads, down_first = lax.optimization_barrier((weight_grads, down_first))
    table_part = jnp.dot(diagonals[:, 0, rows:], bucket_match, precision=HIGHEST)
    table_line = lax.dynamic_update_slice(
        jnp.zeros((count * group, buckets), F32), table_part, (here * group, 0)
    )[:HEADS].reshape(1, HEADS * buckets)
    table_line = jnp.pad(table_line, ((0, 0), (0, width - HEADS * buckets)))
    small = jnp.concatenate([router_grad, gain_moe_grad, table_line], axis=0)
    small = jnp.pad(small, ((0, lanes * SPARE - small.shape[0]), (0, 0))).astype(BF16)
    chunk = 3 * held // lanes
    pack = jnp.concatenate(
        [
            jnp.moveaxis(weight_grads.reshape(3, lanes, held // lanes, width), 1, 0).reshape(
                lanes, chunk, width
            ),
            small.reshape(lanes, SPARE, width),
        ],
        axis=1,
    )
    pack = halve_sum(pack, "expert", bits).astype(BF16)
    pack = jnp.concatenate([pack, proj_rows], axis=0)
    pack = in_order(ring_parts(pack[None], "context"), "context")
    down_second, grads_out = after((down_sent[:, cut:], grads_out), pack)
    down_second = swap(down_second, "context", quarter)
    arrived = context_steps(grads_out)
    up_grad = up_kept.astype(F32) + up_arrived.astype(F32)
    gated = (spread * gates[:, :, None]).reshape(rows, slots)
    output = middle + jnp.dot(
        gated, out_returns.reshape(slots, width).astype(F32), precision=HIGHEST
    )
    half = width // 2
    near = jnp.stack(
        [
            double_gather(pack[:, :, :half], "expert", bits[:0:-1]),
            double_gather(pack[:, :, half:], "expert", bits[1:]),
        ]
    )
    near, arrived, down_second = lax.optimization_barrier((near, arrived, down_second))
    far = swap(near, "expert", bits[0])
    down_arrived = jnp.concatenate([down_first, down_second], axis=1)
    down_grad = down_kept.astype(F32) + down_arrived.astype(F32)
    up_grad = halve_sum(up_grad, "context", low_bits, BF16)
    down_grad = halve_sum(down_grad, "context", low_bits, BF16)
    grad_query, grad_key, grad_value, grad_proj, small, gain_attn_total = assemble(
        own[None], near, far, w_query, w_key, w_value, bits, chunk
    )
    gain_attn_total = gain_attn_total[:, 0] / gain_attn
    router_total = small[:experts].T
    gain_moe_total = small[experts]
    table_total = small[experts + 1, : HEADS * buckets].reshape(HEADS, buckets).T
    normed_grads = 0.0
    for j, weight in enumerate((w_query, w_key, w_value)):
        part = arrived[:, j].reshape(count * held, rows)[:width]
        normed_grads = normed_grads + dot(part, weight, ((0,), (1,)))
    attention_scale = lax.rsqrt(jnp.mean(source * source, axis=1, keepdims=True) + EPSILON)
    token_norm_grads, unused = normalize_back(normed_grads, source, attention_scale, gain_attn)
    token_grads = (middle_grads + token_norm_grads).astype(BF16)
    return (
        output.astype(BF16),
        token_grads,
        gain_attn_total,
        grad_query,
        grad_key,
        grad_value,
        grad_proj,
        table_total,
        gain_moe_total,
        router_total,
        up_grad[None],
        down_grad[None],
    )


def solution(mesh):
    return jax.shard_map(
        shards,
        mesh=mesh,
        in_specs=(
            P(("expert", "context"), None),
            P(),
            P(),
            P(),
            P(),
            P(),
            P(),
            P(),
            P(),
            P("expert", None, None),
            P("expert", None, None),
            P(("expert", "context"), None),
            P(),
            P(("expert", "context"), None),
        ),
        out_specs=(
            P(("expert", "context"), None),
            P(("expert", "context"), None),
            P(),
            P(),
            P(),
            P(),
            P(),
            P(),
            P(),
            P(),
            P("expert", None, "context"),
            P("expert", "context", None),
        ),
        check_vma=False,
    )
```

profile of v0, /device:TPU:0, one launch (start us, length us, event | category | flops | bytes accessed | tf_op | source)
XLA Modules:
  0.0 374.9 jit_solution(157544820070686379)
XLA Ops:
  0.7 5.1 %collective-permute-start.1 = (bf16[256,768]{1,0:T(8,128)(2,1)}, bf16[256,768]{1,0:T(8,128)(2,1)S(1)}, u32[]{:S(2)}, u32[]{:S(2)}) collective-permute-start(bf16[256,768]{1,0:T(8,128)(2,1)} %param.14), channel_id=1, source_target_pairs={{0,3},{1,0},{2,1},{3,2},{4,7},{5,4},{6,5},{7,6},{8,11},{9,8},{10,9... | collective-permute-start | bytes 1179656 | tf_op jit(solution)/shard_map/ppermute | solution.py:41
  13.2 1.8 convolution_convert_fusion.3
  17.1 3.7 all-to-all-start
  20.9 13.4 %collective-permute-done = bf16[256,768]{1,0:T(8,128)(2,1)} collective-permute-done((bf16[256,768]{1,0:T(8,128)(2,1)S(1)}, bf16[256,768]{1,0:T(8,128)(2,1)}, u32[]{:S(2)}, u32[]{:S(2)}) %collective-permute-start) | collective-permute-done | bytes 393248 | tf_op jit(solution)/shard_map/ppermute | solution.py:41
  38.8 8.2 %collective-permute-done.2 = bf16[256,768]{1,0:T(8,128)(2,1)} collective-permute-done((bf16[256,768]{1,0:T(8,128)(2,1)}, bf16[256,768]{1,0:T(8,128)(2,1)}, u32[]{:S(2)}, u32[]{:S(2)}) %collective-permute-start.2) | collective-permute-done | bytes 393248 | tf_op jit(solution)/shard_map/ppermute | solution.py:41
  47.0 1.8 constant_dynamic-update-slice_fusion.16.tokens
  50.5 2.9 collective-permute-start.4
  53.4 10.7 %attend.1 = (bf16[1024,768]{1,0:T(8,128)(2,1)}, bf16[3,192,1024]{2,1,0:T(8,128)(2,1)}, bf16[4,192,256]{2,1,0:T(8,128)(2,1)}, f32[3,64,1024]{2,1,0:T(8,128)}, f32[3,1,1024]{2,1,0:T(1,128)}) custom-call(bf16[1024,768]{1,0:T(8,128)(2,1)} %constant_dynamic-update-slice_fusion.16.tokens, f32[1,768]{1,0:T(1,128)} %broadcast_in_dim.122.gain, ...), custom_call_target="tpu_custom_call" | custom-call | flops 2113929216 | bytes 6291456 | tf_op jit(solution)/shard_map/attend/pallas_call | solution.py:314
  64.1 2.4 collective-permute-done.4
  71.5 1.8 convolution_convert_fusion.1
  74.6 4.4 %all-to-all-start.1 = ((bf16[8,136,768]{2,1,0:T(8,128)(2,1)}), bf16[8,136,768]{2,1,0:T(8,128)(2,1)}, u32[]{:S(2)}, u32[]{:S(2)}) async-start(bf16[8,136,768]{2,1,0:T(8,128)(2,1)} %fusion.3), calls=%async_computation.1 | async-start | bytes 3342336 | tf_op jit(solution)/shard_map/all_to_all | solution.py:611
  79.0 1.9 collective-permute-start.6
  80.9 2.0 collective-permute-start.7
  82.9 3.8 %collective-permute-done.6 = bf16[1,192,256]{2,1,0:T(8,128)(2,1)S(1)} collective-permute-done((bf16[1,192,256]{2,1,0:T(8,128)(2,1)}, bf16[1,192,256]{2,1,0:T(8,128)(2,1)S(1)}, u32[]{:S(2)}, u32[]{:S(2)}) %collective-permute-start.6) | collective-permute-done | bytes 98336 | tf_op jit(solution)/shard_map/ppermute | solution.py:41
  90.6 2.0 convolution_convert_fusion.2
  92.6 8.6 %all-to-all-done.1.other_upstream = bf16[8,136,768]{2,1,0:T(8,128)(2,1)} async-done(((bf16[8,136,768]{2,1,0:T(8,128)(2,1)}), bf16[8,136,768]{2,1,0:T(8,128)(2,1)}, u32[]{:S(2)}, u32[]{:S(2)}) %all-to-all-start.1) | async-done | bytes 1671200 | tf_op jit(solution)/shard_map/all_to_all | solution.py:611
  101.1 16.2 %all-to-all-start.2 = ((bf16[8,128,768]{2,1,0:T(8,128)(2,1)}), bf16[8,128,768]{2,1,0:T(8,128)(2,1)S(1)}, u32[]{:S(2)}, u32[]{:S(2)}) async-start(bf16[8,128,768]{2,1,0:T(8,128)(2,1)} %bitcast.181), calls=%async_computation.2 | async-start | bytes 3145728 | tf_op jit(solution)/shard_map/all_to_all | solution.py:611
  120.7 2.9 collective-permute-start.8
  129.5 12.1 %collective-permute-done.8 = bf16[256,768]{1,0:T(8,128)(2,1)} collective-permute-done((bf16[256,768]{1,0:T(8,128)(2,1)S(1)}, bf16[256,768]{1,0:T(8,128)(2,1)}, u32[]{:S(2)}, u32[]{:S(2)}) %collective-permute-start.8) | collective-permute-done | bytes 393248 | tf_op jit(solution)/shard_map/ppermute | solution.py:46
  143.8 3.0 convolution_convert_fusion
  146.7 3.9 %all-to-all-start.3 = ((bf16[8,128,768]{2,1,0:T(8,128)(2,1)}), bf16[8,128,768]{2,1,0:T(8,128)(2,1)S(1)}, u32[]{:S(2)}, u32[]{:S(2)}) async-start(bf16[8,128,768]{2,1,0:T(8,128)(2,1)} %bitcast.185), calls=%async_computation.3 | async-start | bytes 3145728 | tf_op jit(solution)/shard_map/all_to_all | solution.py:611
  151.2 26.6 %expert.1 = (bf16[1024,768]{1,0:T(8,128)(2,1)}, bf16[8,136,768]{2,1,0:T(8,128)(2,1)}) custom-call(bf16[1024,768]{1,0:T(8,128)(2,1)} %bitcast.178, bf16[8,136,768]{2,1,0:T(8,128)(2,1)} %copy-done.22, f32[8,1,128]{2,1,0:T(1,128)} %fusion.49.gate.own_gate, bf16[768,3072]{1,0:T(8,128)(2,1)} %bitcast.215, bf16[3072,768]{1,0:T(8,128)(2,1)} %bitcast.218), custom_call_target="tpu_custom_call" | custom-call | flops 24159191040 | bytes 9437184 | tf_op jit(solution)/shard_map/expert/pallas_call | solution.py:386
  178.9 4.2 %all-to-all-start.4 = ((bf16[8,136,768]{2,1,0:T(8,128)(2,1)}), bf16[8,136,768]{2,1,0:T(8,128)(2,1)S(1)}, u32[]{:S(2)}, u32[]{:S(2)}) async-start(bf16[8,136,768]{2,1,0:T(8,128)(2,1)} %get-tuple-element.87), calls=%async_computation.4 | async-start | bytes 3342336 | tf_op jit(solution)/shard_map/all_to_all | solution.py:611
  183.2 1.9 select_reduce_fusion
  186.5 15.1 %expert_grads.2 = (bf16[1,768,768]{2,1,0:T(8,128)(2,1)}, bf16[1,768,768]{2,1,0:T(8,128)(2,1)}) custom-call(s32[1]{0:T(128)} %bitcast.28.index, bf16[1024,768]{1,0:T(8,128)(2,1)} %bitcast.179, bf16[1024,768]{1,0:T(8,128)(2,1)} %bitcast.183, bf16[8,136,768]{2,1,0:T(8,128)(2,1)} %copy-done.22, bf16[8,136,768]{2,1,0:T(8,128)(2,1)} %all-to-all-done.1.other_upstream, ...), custom_call_target="tpu_custom_call" | custom-call | flops 9663676416 | bytes 6291456 | tf_op jit(solution)/shard_map/expert_grads/pallas_call | solution.py:423
  201.5 15.2 %expert_grads.3 = (bf16[1,768,768]{2,1,0:T(8,128)(2,1)}, bf16[1,768,768]{2,1,0:T(8,128)(2,1)}) custom-call(s32[1]{0:T(128)} %bitcast.34.index, bf16[1024,768]{1,0:T(8,128)(2,1)} %bitcast.180, bf16[1024,768]{1,0:T(8,128)(2,1)} %bitcast.184, bf16[8,136,768]{2,1,0:T(8,128)(2,1)} %copy-done.22, bf16[8,136,768]{2,1,0:T(8,128)(2,1)} %all-to-all-done.1.other_upstream, ...), custom_call_target="tpu_custom_call" | custom-call | flops 9663676416 | bytes 6291456 | tf_op jit(solution)/shard_map/expert_grads/pallas_call | solution.py:423
  217.9 6.5 %token_back.1 = (f32[256,768]{1,0:T(8,128)}, bf16[256,768]{1,0:T(8,128)(2,1)}, bf16[768,256]{1,0:T(8,128)(2,1)}, f32[1,768]{1,0:T(1,128)}, f32[8,768]{1,0:T(8,128)}) custom-call(bf16[8,136,768]{2,1,0:T(8,128)(2,1)} %copy-done.6, bf16[256,1024]{1,0:T(8,128)(2,1)} %get-tuple-element.128.dispatch, f32[256,8]{1,0:T(8,128)} %fusion.38.gates, ...), custom_call_target="tpu_custom_call" | custom-call | tf_op jit(solution)/shard_map/token_back/pallas_call | solution.py:580
  226.2 1.9 collective-permute-start.9
  228.3 3.6 collective-permute-start.11
  237.1 4.7 %all-to-all-start.5 = ((bf16[8,128,768]{2,1,0:T(8,128)(2,1)}), bf16[8,128,768]{2,1,0:T(8,128)(2,1)}, u32[]{:S(2)}, u32[]{:S(2)}) async-start(bf16[8,128,768]{2,1,0:T(8,128)(2,1)} %bitcast.198), calls=%async_computation.5 | async-start | bytes 3145728 | tf_op jit(solution)/shard_map/all_to_all | solution.py:611
  244.6 13.0 %attend_back.1 = (bf16[4,3,192,256]{3,2,1,0:T(8,128)(2,1)}, bf16[3,192,768]{2,1,0:T(8,128)(2,1)}, f32[3,1,1280]{2,1,0:T(1,128)}) custom-call(bf16[3,192,1024]{2,1,0:T(8,128)(2,1)} %get-tuple-element.76.qkv, bf16[1024,768]{1,0:T(8,128)(2,1)} %get-tuple-element.77.normed, f32[3,1,1280]{2,1,0:T(1,128)} %broadcast_in_dim.123.bias, ...), custom_call_target="tpu_custom_call" | custom-call | flops 2717908992 | bytes 6291456 | tf_op jit(solution)/shard_map/attend_back/pallas_call | solution.py:348
  260.6 2.1 collective-permute-start.18
  263.4 6.8 %collective-permute-done.18 = bf16[2,96,768]{2,1,0:T(8,128)(2,1)S(1)} collective-permute-done((bf16[2,96,768]{2,1,0:T(8,128)(2,1)S(1)}, bf16[2,96,768]{2,1,0:T(8,128)(2,1)S(1)}, u32[]{:S(2)}, u32[]{:S(2)}) %collective-permute-start.18) | collective-permute-done | bytes 294944 | tf_op jit(solution)/shard_map/ppermute | solution.py:46
  275.1 4.6 %collective-permute-done.19 = bf16[1,96,768]{2,1,0:T(8,128)(2,1)S(1)} collective-permute-done((bf16[1,96,768]{2,1,0:T(8,128)(2,1)S(1)}, bf16[1,96,768]{2,1,0:T(8,128)(2,1)S(1)}, u32[]{:S(2)}, u32[]{:S(2)}) %collective-permute-start.19) | collective-permute-done | bytes 147488 | tf_op jit(solution)/shard_map/ppermute | solution.py:46
  284.6 2.5 collective-permute-start.22
  290.5 3.1 collective-permute-done.16
  293.6 1.8 collective-permute-start.23
  295.4 2.1 collective-permute-start.24
  297.6 3.5 collective-permute-done.23
  302.9 5.3 %collective-permute-done.25 = bf16[1,104,768]{2,1,0:T(8,128)(2,1)S(1)} collective-permute-done((bf16[1,104,768]{2,1,0:T(8,128)(2,1)S(1)}, bf16[1,104,768]{2,1,0:T(8,128)(2,1)S(1)}, u32[]{:S(2)}, u32[]{:S(2)}) %collective-permute-start.25) | collective-permute-done | bytes 159776 | tf_op jit(solution)/shard_map/ppermute | solution.py:41
  312.7 2.3 collective-permute-start.30
  315.0 4.0 %collective-permute-start.32 = (bf16[1,3,192,256]{3,2,1,0:T(8,128)(2,1)}, bf16[1,3,192,256]{3,2,1,0:T(8,128)(2,1)}, u32[]{:S(2)}, u32[]{:S(2)}) collective-permute-start(bf16[1,3,192,256]{3,2,1,0:T(8,128)(2,1)} %get-tuple-element.137), channel_id=1, source_target_pairs={{0,3},{1,0},{2,1},{3,2},{4,7},{5,4},{6,5},{7,6},{8,11},{9,8},{10,9... | collective-permute-start | bytes 884744 | tf_op jit(solution)/shard_map/ppermute | solution.py:41
  322.0 8.1 %collective-permute-done.30 = bf16[1,3,192,256]{3,2,1,0:T(8,128)(2,1)} collective-permute-done((bf16[1,3,192,256]{3,2,1,0:T(8,128)(2,1)}, bf16[1,3,192,256]{3,2,1,0:T(8,128)(2,1)}, u32[]{:S(2)}, u32[]{:S(2)}) %collective-permute-start.30) | collective-permute-done | bytes 294944 | tf_op jit(solution)/shard_map/ppermute | solution.py:41
  337.1 8.1 %collective-permute-done.33 = bf16[1,384,768]{2,1,0:T(8,128)(2,1)S(1)} collective-permute-done((bf16[1,384,768]{2,1,0:T(8,128)(2,1)}, bf16[1,384,768]{2,1,0:T(8,128)(2,1)S(1)}, u32[]{:S(2)}, u32[]{:S(2)}) %collective-permute-start.33) | collective-permute-done | bytes 589856 | tf_op jit(solution)/shard_map/ppermute | solution.py:46
  345.3 3.0 convert_add_fusion.1
  348.3 4.3 %fusion.6 = bf16[256,768]{1,0:T(8,128)(2,1)} fusion(f32[256,768]{1,0:T(8,128)S(1)} %copy-done.5, bf16[8,128,768]{2,1,0:T(8,128)(2,1)} %all-to-all-done.5, f32[256,8]{0,1:T(8,128)S(1)} %copy.73, s32[256,8]{0,1:T(8,128)S(1)} %copy-done.39, pred[256,8]{0,1:T(8,128)(4,1)S(1)} %fusion.44), kind=kOutput, calls=%fused_computation.23 | convolution fusion | flops 2417623040 | bytes 2770944 | tf_op jit(solution)/shard_map/dot_general | solution.py:856
  357.7 2.7 convert_add_fusion
  361.9 6.9 %assemble.1 = (f32[768,768]{1,0:T(8,128)}, f32[768,768]{1,0:T(8,128)}, f32[768,768]{1,0:T(8,128)}, f32[768,768]{1,0:T(8,128)}, f32[64,768]{1,0:T(8,128)}, /*index=5*/f32[768,1]{1,0:T(8,128)}) custom-call(s32[1]{0:T(128)} %bitcast.70.index, bf16[2,2,2,4,104,384]{5,4,3,2,1,0:T(8,128)(2,1)} %copy-done.2, bf16[2,2,2,4,104,384]{5,4,3,2,1,0:T(8,128)(2,1)} %copy-done.21, ...), custom_call_target="tpu_custom_call" | custom-call | tf_op jit(solution)/shard_map/assemble/pallas_call | solution.py:516
  (266 shorter events, 96.8 us)
Async XLA Ops:
  0.6 48.2 %copy-start = (f32[32,12]{0,1:T(8,128)S(1)}, f32[32,12]{0,1:T(8,128)}, u32[]{:S(2)}) copy-start(f32[32,12]{0,1:T(8,128)} %param.20) | copy-start | bytes 4612
  0.7 15.7 %collective-permute-start.1 = (bf16[256,768]{1,0:T(8,128)(2,1)}, bf16[256,768]{1,0:T(8,128)(2,1)S(1)}, u32[]{:S(2)}, u32[]{:S(2)}) collective-permute-start(bf16[256,768]{1,0:T(8,128)(2,1)} %param.14), channel_id=1, source_target_pairs={{0,3},{1,0},{2,1},{3,2},{4,7},{5,4},{6,5},{7,6},{8,11},{9,8},{10,9... | collective-permute-start | bytes 1179656 | tf_op jit(solution)/shard_map/ppermute | solution.py:41
  17.1 49.5 %all-to-all-start = ((bf16[8,136,768]{2,1,0:T(8,128)(2,1)}), bf16[8,136,768]{2,1,0:T(8,128)(2,1)S(1)}, u32[]{:S(2)}, u32[]{:S(2)}) async-start(bf16[8,136,768]{2,1,0:T(8,128)(2,1)} %fusion.2), calls=%async_computation | async-start | bytes 3342336 | tf_op jit(solution)/shard_map/all_to_all | solution.py:611
  20.8 13.4 %collective-permute-start = (bf16[256,768]{1,0:T(8,128)(2,1)S(1)}, bf16[256,768]{1,0:T(8,128)(2,1)}, u32[]{:S(2)}, u32[]{:S(2)}) collective-permute-start(bf16[256,768]{1,0:T(8,128)(2,1)S(1)} %copy-done.3), channel_id=1, source_target_pairs={{0,1},{1,2},{2,3},{3,0},{4,5},{5,6},{6,7},{7,4},{8,9},{9,10},{10,1... | collective-permute-start | bytes 1179656 | tf_op jit(solution)/shard_map/ppermute | solution.py:41
  34.2 12.8 %collective-permute-start.2 = (bf16[256,768]{1,0:T(8,128)(2,1)}, bf16[256,768]{1,0:T(8,128)(2,1)}, u32[]{:S(2)}, u32[]{:S(2)}) collective-permute-start(bf16[256,768]{1,0:T(8,128)(2,1)} %collective-permute-done), channel_id=1, source_target_pairs={{0,1},{1,2},{2,3},{3,0},{4,5},{5,6},{6,7},{7,4},{8,9},{9,10},{10,1... | collective-permute-start | bytes 1179656 | tf_op jit(solution)/shard_map/ppermute | solution.py:41
  35.5 13.3 %copy-start.42 = (s32[1024]{0:T(1024)S(1)}, s32[1024]{0:T(1024)}, u32[]{:S(2)}) copy-start(s32[1024]{0:T(1024)} %param.26) | copy-start | bytes 12292
  35.5 13.8 %copy-start.35 = (f32[768]{0:T(1024)S(1)}, f32[768]{0:T(1024)}, u32[]{:S(2)}) copy-start(f32[768]{0:T(1024)} %param.15) | copy-start | bytes 9220
  35.5 15.0 %copy-start.41 = (s32[256,2]{0,1:T(2,128)S(1)}, s32[256,2]{0,1:T(2,128)}, u32[]{:S(2)}) copy-start(s32[256,2]{0,1:T(2,128)} %param.25) | copy-start | bytes 6148
  48.8 17.7 %collective-permute-start.3 = (bf16[256,768]{1,0:T(8,128)(2,1)}, bf16[256,768]{1,0:T(8,128)(2,1)}, u32[]{:S(2)}, u32[]{:S(2)}) collective-permute-start(bf16[256,768]{1,0:T(8,128)(2,1)} %cotangent.1), channel_id=1, source_target_pairs={{0,2},{1,3},{2,0},{3,1},{4,6},{5,7},{6,4},{7,5},{8,10},{9,11},{10,... | collective-permute-start | bytes 1179656 | tf_op jit(solution)/shard_map/ppermute | solution.py:46
  50.5 16.0 %collective-permute-start.4 = (s32[2,256]{1,0:T(2,128)S(1)}, s32[2,256]{1,0:T(2,128)S(1)}, u32[]{:S(2)}, u32[]{:S(2)}) collective-permute-start(s32[2,256]{1,0:T(2,128)S(1)} %bitcast.213), channel_id=1, source_target_pairs={{0,2},{1,3},{2,0},{3,1},{4,6},{5,7},{6,4},{7,5},{8,10},{9,11},{10,... | collective-permute-start | bytes 6152 | tf_op jit(solution)/shard_map/ppermute | solution.py:46
  69.7 13.2 %collective-permute-start.5 = (bf16[1,192,256]{2,1,0:T(8,128)(2,1)}, bf16[1,192,256]{2,1,0:T(8,128)(2,1)S(1)}, u32[]{:S(2)}, u32[]{:S(2)}) collective-permute-start(bf16[1,192,256]{2,1,0:T(8,128)(2,1)} %get-tuple-element.157), channel_id=1, source_target_pairs={{0,2},{1,3},{2,0},{3,1},{4,6},{5,7},{6,4},{7,5},{8,10},{9,11},{10,... | collective-permute-start | bytes 294920 | tf_op jit(solution)/shard_map/ppermute | solution.py:41
  74.6 14.2 %copy-start.13 = (bf16[768,768]{1,0:T(8,128)(2,1)S(1)}, bf16[768,768]{1,0:T(8,128)(2,1)}, u32[]{:S(2)}) copy-start(bf16[768,768]{1,0:T(8,128)(2,1)} %proj.1) | copy-start | bytes 3538948
  74.6 26.5 %all-to-all-start.1 = ((bf16[8,136,768]{2,1,0:T(8,128)(2,1)}), bf16[8,136,768]{2,1,0:T(8,128)(2,1)}, u32[]{:S(2)}, u32[]{:S(2)}) async-start(bf16[8,136,768]{2,1,0:T(8,128)(2,1)} %fusion.3), calls=%async_computation.1 | async-start | bytes 3342336 | tf_op jit(solution)/shard_map/all_to_all | solution.py:611
  79.0 7.7 %collective-permute-start.6 = (bf16[1,192,256]{2,1,0:T(8,128)(2,1)}, bf16[1,192,256]{2,1,0:T(8,128)(2,1)S(1)}, u32[]{:S(2)}, u32[]{:S(2)}) collective-permute-start(bf16[1,192,256]{2,1,0:T(8,128)(2,1)} %get-tuple-element.156), channel_id=1, source_target_pairs={{0,1},{1,2},{2,3},{3,0},{4,5},{5,6},{6,7},{7,4},{8,9},{9,10},{10,1... | collective-permute-start | bytes 294920 | tf_op jit(solution)/shard_map/ppermute | solution.py:41
  80.9 7.1 %collective-permute-start.7 = (bf16[1,192,256]{2,1,0:T(8,128)(2,1)}, bf16[1,192,256]{2,1,0:T(8,128)(2,1)S(1)}, u32[]{:S(2)}, u32[]{:S(2)}) collective-permute-start(bf16[1,192,256]{2,1,0:T(8,128)(2,1)} %get-tuple-element.155), channel_id=1, source_target_pairs={{0,3},{1,0},{2,1},{3,2},{4,7},{5,4},{6,5},{7,6},{8,11},{9,8},{10,9... | collective-permute-start | bytes 294920 | tf_op jit(solution)/shard_map/ppermute | solution.py:41
  90.6 33.0 %copy-start.12 = (bf16[256,768]{1,0:T(8,128)(2,1)}, bf16[256,768]{1,0:T(8,128)(2,1)S(1)}, u32[]{:S(2)}) copy-start(bf16[256,768]{1,0:T(8,128)(2,1)S(1)} %multiply_convert_fusion.routed) | copy-start | bytes 1179652
  101.1 40.5 %all-to-all-start.2 = ((bf16[8,128,768]{2,1,0:T(8,128)(2,1)}), bf16[8,128,768]{2,1,0:T(8,128)(2,1)S(1)}, u32[]{:S(2)}, u32[]{:S(2)}) async-start(bf16[8,128,768]{2,1,0:T(8,128)(2,1)} %bitcast.181), calls=%async_computation.2 | async-start | bytes 3145728 | tf_op jit(solution)/shard_map/all_to_all | solution.py:611
  120.7 20.9 %collective-permute-start.8 = (bf16[256,768]{1,0:T(8,128)(2,1)S(1)}, bf16[256,768]{1,0:T(8,128)(2,1)}, u32[]{:S(2)}, u32[]{:S(2)}) collective-permute-start(bf16[256,768]{1,0:T(8,128)(2,1)S(1)} %multiply_convert_fusion.routed), channel_id=1, source_target_pairs={{0,2},{1,3},{2,0},{3,1},{4,6},{5,7},{6,4},{7,5},{8,10},{9,11},{10,... | collective-permute-start | bytes 1179656 | tf_op jit(solution)/shard_map/ppermute | solution.py:46
  146.7 31.1 %all-to-all-start.3 = ((bf16[8,128,768]{2,1,0:T(8,128)(2,1)}), bf16[8,128,768]{2,1,0:T(8,128)(2,1)S(1)}, u32[]{:S(2)}, u32[]{:S(2)}) async-start(bf16[8,128,768]{2,1,0:T(8,128)(2,1)} %bitcast.185), calls=%async_computation.3 | async-start | bytes 3145728 | tf_op jit(solution)/shard_map/all_to_all | solution.py:611
  178.9 37.8 %all-to-all-start.4 = ((bf16[8,136,768]{2,1,0:T(8,128)(2,1)}), bf16[8,136,768]{2,1,0:T(8,128)(2,1)S(1)}, u32[]{:S(2)}, u32[]{:S(2)}) async-start(bf16[8,136,768]{2,1,0:T(8,128)(2,1)} %get-tuple-element.87), calls=%async_computation.4 | async-start | bytes 3342336 | tf_op jit(solution)/shard_map/all_to_all | solution.py:611
  201.5 43.1 %collective-permute-start.12 = (bf16[1,768,768]{2,1,0:T(8,128)(2,1)}, bf16[1,768,768]{2,1,0:T(8,128)(2,1)}, u32[]{:S(2)}, u32[]{:S(2)}) collective-permute-start(bf16[1,768,768]{2,1,0:T(8,128)(2,1)} %get-tuple-element.97), channel_id=1, source_target_pairs={{0,1},{1,0},{2,3},{3,2},{4,5},{5,4},{6,7},{7,6},{8,9},{9,8},{10,11... | collective-permute-start | bytes 3538952 | tf_op jit(solution)/shard_map/ppermute | solution.py:46
  217.9 14.0 %copy-start.19 = (bf16[4,192,256]{2,1,0:T(8,128)(2,1)S(1)}, bf16[4,192,256]{2,1,0:T(8,128)(2,1)}, u32[]{:S(2)}) copy-start(bf16[4,192,256]{2,1,0:T(8,128)(2,1)} %copy-done.18) | copy-start | bytes 1179652
  226.2 10.8 %collective-permute-start.9 = (bf16[1,192,256]{2,1,0:T(8,128)(2,1)S(1)}, bf16[1,192,256]{2,1,0:T(8,128)(2,1)}, u32[]{:S(2)}, u32[]{:S(2)}) collective-permute-start(bf16[1,192,256]{2,1,0:T(8,128)(2,1)S(1)} %get-tuple-element.153), channel_id=1, source_target_pairs={{0,2},{1,3},{2,0},{3,1},{4,6},{5,7},{6,4},{7,5},{8,10},{9,11},{10,... | collective-permute-start | bytes 294920 | tf_op jit(solution)/shard_map/ppermute | solution.py:41
  228.1 15.2 %collective-permute-start.10 = (bf16[1,192,256]{2,1,0:T(8,128)(2,1)}, bf16[1,192,256]{2,1,0:T(8,128)(2,1)S(1)}, u32[]{:S(2)}, u32[]{:S(2)}) collective-permute-start(bf16[1,192,256]{2,1,0:T(8,128)(2,1)} %get-tuple-element.152), channel_id=1, source_target_pairs={{0,1},{1,2},{2,3},{3,0},{4,5},{5,6},{6,7},{7,4},{8,9},{9,10},{10,1... | collective-permute-start | bytes 294920 | tf_op jit(solution)/shard_map/ppermute | solution.py:41
  228.3 15.7 %collective-permute-start.11 = (bf16[1,192,256]{2,1,0:T(8,128)(2,1)}, bf16[1,192,256]{2,1,0:T(8,128)(2,1)S(1)}, u32[]{:S(2)}, u32[]{:S(2)}) collective-permute-start(bf16[1,192,256]{2,1,0:T(8,128)(2,1)} %get-tuple-element.151), channel_id=1, source_target_pairs={{0,3},{1,0},{2,1},{3,2},{4,7},{5,4},{6,5},{7,6},{8,11},{9,8},{10,9... | collective-permute-start | bytes 294920 | tf_op jit(solution)/shard_map/ppermute | solution.py:41
  234.4 24.0 %collective-permute-start.17 = (bf16[4,96,768]{2,1,0:T(8,128)(2,1)}, bf16[4,96,768]{2,1,0:T(8,128)(2,1)S(1)}, u32[]{:S(2)}, u32[]{:S(2)}) collective-permute-start(bf16[4,96,768]{2,1,0:T(8,128)(2,1)} %dynamic-slice_bitcast_fusion), channel_id=1, source_target_pairs={{0,4},{4,0},{8,12},{12,8},{16,20},{20,16},{24,28},{28,24},{1,5},{5... | collective-permute-start | bytes 1769480 | tf_op jit(solution)/shard_map/ppermute | solution.py:46
  237.1 34.2 %all-to-all-start.5 = ((bf16[8,128,768]{2,1,0:T(8,128)(2,1)}), bf16[8,128,768]{2,1,0:T(8,128)(2,1)}, u32[]{:S(2)}, u32[]{:S(2)}) async-start(bf16[8,128,768]{2,1,0:T(8,128)(2,1)} %bitcast.198), calls=%async_computation.5 | async-start | bytes 3145728 | tf_op jit(solution)/shard_map/all_to_all | solution.py:611
  244.6 26.7 %collective-permute-start.13 = (bf16[1,384,768]{2,1,0:T(8,128)(2,1)}, bf16[1,384,768]{2,1,0:T(8,128)(2,1)}, u32[]{:S(2)}, u32[]{:S(2)}) collective-permute-start(bf16[1,384,768]{2,1,0:T(8,128)(2,1)} %get-tuple-element.107), channel_id=1, source_target_pairs={{0,1},{1,0},{2,3},{3,2},{4,5},{5,4},{6,7},{7,6},{8,9},{9,8},{10,11... | collective-permute-start | bytes 1769480 | tf_op jit(solution)/shard_map/ppermute | solution.py:46
  260.6 9.5 %collective-permute-start.18 = (bf16[2,96,768]{2,1,0:T(8,128)(2,1)S(1)}, bf16[2,96,768]{2,1,0:T(8,128)(2,1)S(1)}, u32[]{:S(2)}, u32[]{:S(2)}) collective-permute-start(bf16[2,96,768]{2,1,0:T(8,128)(2,1)S(1)} %fusion.33), channel_id=1, source_target_pairs={{0,16},{4,20},{8,24},{12,28},{16,0},{20,4},{24,8},{28,12},{1,17},{... | collective-permute-start | bytes 884744 | tf_op jit(solution)/shard_map/ppermute | solution.py:46
  273.3 6.4 %collective-permute-start.14 = (bf16[4,80,768]{2,1,0:T(8,128)(2,1)}, bf16[4,80,768]{2,1,0:T(8,128)(2,1)}, u32[]{:S(2)}, u32[]{:S(2)}) collective-permute-start(bf16[4,80,768]{2,1,0:T(8,128)(2,1)} %fusion.30), channel_id=1, source_target_pairs={{0,4},{4,0},{8,12},{12,8},{16,20},{20,16},{24,28},{28,24},{1,5},{5... | collective-permute-start | bytes 1474568 | tf_op jit(solution)/shard_map/ppermute | solution.py:46
  273.4 6.3 %collective-permute-start.19 = (bf16[1,96,768]{2,1,0:T(8,128)(2,1)S(1)}, bf16[1,96,768]{2,1,0:T(8,128)(2,1)S(1)}, u32[]{:S(2)}, u32[]{:S(2)}) collective-permute-start(bf16[1,96,768]{2,1,0:T(8,128)(2,1)S(1)} %dynamic-slice_convert_fusion.2), channel_id=1, source_target_pairs={{0,8},{4,12},{8,0},{12,4},{16,24},{20,28},{24,16},{28,20},{1,9},{5... | collective-permute-start | bytes 442376 | tf_op jit(solution)/shard_map/ppermute | solution.py:46
  280.9 7.7 %collective-permute-start.15 = (bf16[2,80,768]{2,1,0:T(8,128)(2,1)S(1)}, bf16[2,80,768]{2,1,0:T(8,128)(2,1)S(1)}, u32[]{:S(2)}, u32[]{:S(2)}) collective-permute-start(bf16[2,80,768]{2,1,0:T(8,128)(2,1)S(1)} %fusion.36), channel_id=1, source_target_pairs={{0,16},{4,20},{8,24},{12,28},{16,0},{20,4},{24,8},{28,12},{1,17},{... | collective-permute-start | bytes 737288 | tf_op jit(solution)/shard_map/ppermute | solution.py:46
  282.7 5.8 %collective-permute-start.20 = (bf16[1,24,768]{2,1,0:T(8,128)(2,1)S(1)}, bf16[1,24,768]{2,1,0:T(8,128)(2,1)S(1)}, u32[]{:S(2)}, u32[]{:S(2)}) collective-permute-start(bf16[1,24,768]{2,1,0:T(8,128)(2,1)S(1)} %get-tuple-element.161), channel_id=1, source_target_pairs={{0,2},{1,3},{2,0},{3,1},{4,6},{5,7},{6,4},{7,5},{8,10},{9,11},{10,... | collective-permute-start | bytes 110600 | tf_op jit(solution)/shard_map/ppermute | solution.py:41
  283.2 7.2 %collective-permute-start.21 = (bf16[1,24,768]{2,1,0:T(8,128)(2,1)S(1)}, bf16[1,24,768]{2,1,0:T(8,128)(2,1)S(1)}, u32[]{:S(2)}, u32[]{:S(2)}) collective-permute-start(bf16[1,24,768]{2,1,0:T(8,128)(2,1)S(1)} %get-tuple-element.160), channel_id=1, source_target_pairs={{0,1},{1,2},{2,3},{3,0},{4,5},{5,6},{6,7},{7,4},{8,9},{9,10},{10,1... | collective-permute-start | bytes 110600 | tf_op jit(solution)/shard_map/ppermute | solution.py:41
  284.6 5.8 %collective-permute-start.22 = (bf16[1,24,768]{2,1,0:T(8,128)(2,1)S(1)}, bf16[1,24,768]{2,1,0:T(8,128)(2,1)S(1)}, u32[]{:S(2)}, u32[]{:S(2)}) collective-permute-start(bf16[1,24,768]{2,1,0:T(8,128)(2,1)S(1)} %get-tuple-element.159), channel_id=1, source_target_pairs={{0,3},{1,0},{2,1},{3,2},{4,7},{5,4},{6,5},{7,6},{8,11},{9,8},{10,9... | collective-permute-start | bytes 110600 | tf_op jit(solution)/shard_map/ppermute | solution.py:41
  288.7 4.9 %collective-permute-start.16 = (bf16[1,80,768]{2,1,0:T(8,128)(2,1)S(1)}, bf16[1,80,768]{2,1,0:T(8,128)(2,1)S(1)}, u32[]{:S(2)}, u32[]{:S(2)}) collective-permute-start(bf16[1,80,768]{2,1,0:T(8,128)(2,1)S(1)} %dynamic-slice_convert_fusion.3), channel_id=1, source_target_pairs={{0,8},{4,12},{8,0},{12,4},{16,24},{20,28},{24,16},{28,20},{1,9},{5... | collective-permute-start | bytes 368648 | tf_op jit(solution)/shard_map/ppermute | solution.py:46
  293.6 7.5 %collective-permute-start.23 = (bf16[1,104,768]{2,1,0:T(8,128)(2,1)S(1)}, bf16[1,104,768]{2,1,0:T(8,128)(2,1)S(1)}, u32[]{:S(2)}, u32[]{:S(2)}) collective-permute-start(bf16[1,104,768]{2,1,0:T(8,128)(2,1)S(1)} %maximum_bitcast_fusion.2), channel_id=1, source_target_pairs={{0,1},{1,2},{2,3},{3,0},{4,5},{5,6},{6,7},{7,4},{8,9},{9,10},{10,1... | collective-permute-start | bytes 479240 | tf_op jit(solution)/shard_map/ppermute | solution.py:41
  295.4 7.5 %collective-permute-start.24 = (bf16[1,104,768]{2,1,0:T(8,128)(2,1)S(1)}, bf16[1,104,768]{2,1,0:T(8,128)(2,1)S(1)}, u32[]{:S(2)}, u32[]{:S(2)}) collective-permute-start(bf16[1,104,768]{2,1,0:T(8,128)(2,1)S(1)} %maximum_bitcast_fusion.2), channel_id=1, source_target_pairs={{0,3},{1,0},{2,1},{3,2},{4,7},{5,4},{6,5},{7,6},{8,11},{9,8},{10,9... | collective-permute-start | bytes 479240 | tf_op jit(solution)/shard_map/ppermute | solution.py:41
  301.1 7.1 %collective-permute-start.25 = (bf16[1,104,768]{2,1,0:T(8,128)(2,1)S(1)}, bf16[1,104,768]{2,1,0:T(8,128)(2,1)S(1)}, u32[]{:S(2)}, u32[]{:S(2)}) collective-permute-start(bf16[1,104,768]{2,1,0:T(8,128)(2,1)S(1)} %collective-permute-done.23), channel_id=1, source_target_pairs={{0,1},{1,2},{2,3},{3,0},{4,5},{5,6},{6,7},{7,4},{8,9},{9,10},{10,1... | collective-permute-start | bytes 479240 | tf_op jit(solution)/shard_map/ppermute | solution.py:41
  308.3 10.7 %collective-permute-start.28 = (bf16[4,104,384]{2,1,0:T(8,128)(2,1)S(1)}, bf16[4,104,384]{2,1,0:T(8,128)(2,1)S(1)}, u32[]{:S(2)}, u32[]{:S(2)}) collective-permute-start(bf16[4,104,384]{2,1,0:T(8,128)(2,1)S(1)} %get-tuple-element.147), channel_id=1, source_target_pairs={{0,16},{4,20},{8,24},{12,28},{16,0},{20,4},{24,8},{28,12},{1,17},{... | collective-permute-start | bytes 958472 | tf_op jit(solution)/shard_map/ppermute | solution.py:46
  310.1 9.9 %collective-permute-start.26 = (bf16[4,104,384]{2,1,0:T(8,128)(2,1)S(1)}, bf16[4,104,384]{2,1,0:T(8,128)(2,1)S(1)}, u32[]{:S(2)}, u32[]{:S(2)}) collective-permute-start(bf16[4,104,384]{2,1,0:T(8,128)(2,1)S(1)} %get-tuple-element.148), channel_id=1, source_target_pairs={{0,8},{4,12},{8,0},{12,4},{16,24},{20,28},{24,16},{28,20},{1,9},{5... | collective-permute-start | bytes 958472 | tf_op jit(solution)/shard_map/ppermute | solution.py:46
  312.7 17.3 %collective-permute-start.30 = (bf16[1,3,192,256]{3,2,1,0:T(8,128)(2,1)}, bf16[1,3,192,256]{3,2,1,0:T(8,128)(2,1)}, u32[]{:S(2)}, u32[]{:S(2)}) collective-permute-start(bf16[1,3,192,256]{3,2,1,0:T(8,128)(2,1)} %get-tuple-element.139), channel_id=1, source_target_pairs={{0,2},{1,3},{2,0},{3,1},{4,6},{5,7},{6,4},{7,5},{8,10},{9,11},{10,... | collective-permute-start | bytes 884744 | tf_op jit(solution)/shard_map/ppermute | solution.py:41
  315.0 17.2 %collective-permute-start.31 = (bf16[1,3,192,256]{3,2,1,0:T(8,128)(2,1)}, bf16[1,3,192,256]{3,2,1,0:T(8,128)(2,1)}, u32[]{:S(2)}, u32[]{:S(2)}) collective-permute-start(bf16[1,3,192,256]{3,2,1,0:T(8,128)(2,1)} %get-tuple-element.138), channel_id=1, source_target_pairs={{0,1},{1,2},{2,3},{3,0},{4,5},{5,6},{6,7},{7,4},{8,9},{9,10},{10,1... | collective-permute-start | bytes 884744 | tf_op jit(solution)/shard_map/ppermute | solution.py:41
  315.0 18.2 %collective-permute-start.32 = (bf16[1,3,192,256]{3,2,1,0:T(8,128)(2,1)}, bf16[1,3,192,256]{3,2,1,0:T(8,128)(2,1)}, u32[]{:S(2)}, u32[]{:S(2)}) collective-permute-start(bf16[1,3,192,256]{3,2,1,0:T(8,128)(2,1)} %get-tuple-element.137), channel_id=1, source_target_pairs={{0,3},{1,0},{2,1},{3,2},{4,7},{5,4},{6,5},{7,6},{8,11},{9,8},{10,9... | collective-permute-start | bytes 884744 | tf_op jit(solution)/shard_map/ppermute | solution.py:41
  319.9 14.3 %collective-permute-start.29 = (bf16[2,4,104,384]{3,2,1,0:T(8,128)(2,1)}, bf16[2,4,104,384]{3,2,1,0:T(8,128)(2,1)}, u32[]{:S(2)}, u32[]{:S(2)}) collective-permute-start(bf16[2,4,104,384]{3,2,1,0:T(8,128)(2,1)} %get-tuple-element.150), channel_id=1, source_target_pairs={{0,8},{4,12},{8,0},{12,4},{16,24},{20,28},{24,16},{28,20},{1,9},{5... | collective-permute-start | bytes 1916936 | tf_op jit(solution)/shard_map/ppermute | solution.py:46
  321.1 14.4 %collective-permute-start.27 = (bf16[2,4,104,384]{3,2,1,0:T(8,128)(2,1)}, bf16[2,4,104,384]{3,2,1,0:T(8,128)(2,1)}, u32[]{:S(2)}, u32[]{:S(2)}) collective-permute-start(bf16[2,4,104,384]{3,2,1,0:T(8,128)(2,1)} %get-tuple-element.144), channel_id=1, source_target_pairs={{0,16},{4,20},{8,24},{12,28},{16,0},{20,4},{24,8},{28,12},{1,17},{... | collective-permute-start | bytes 1916936 | tf_op jit(solution)/shard_map/ppermute | solution.py:46
  330.1 15.2 %collective-permute-start.33 = (bf16[1,384,768]{2,1,0:T(8,128)(2,1)}, bf16[1,384,768]{2,1,0:T(8,128)(2,1)S(1)}, u32[]{:S(2)}, u32[]{:S(2)}) collective-permute-start(bf16[1,384,768]{2,1,0:T(8,128)(2,1)} %get-tuple-element.115), channel_id=1, source_target_pairs={{0,1},{1,0},{2,3},{3,2},{4,5},{5,4},{6,7},{7,6},{8,9},{9,8},{10,11... | collective-permute-start | bytes 1769480 | tf_op jit(solution)/shard_map/ppermute | solution.py:46
  345.3 15.2 %collective-permute-start.34 = (bf16[2,2,2,4,104,384]{5,4,3,2,1,0:T(8,128)(2,1)S(1)}, bf16[2,2,2,4,104,384]{5,4,3,2,1,0:T(8,128)(2,1)S(1)}, u32[]{:S(2)}, u32[]{:S(2)}) collective-permute-start(bf16[2,2,2,4,104,384]{5,4,3,2,1,0:T(8,128)(2,1)S(1)} %pad_maximum_fusion.near), channel_id=1, source_target_pairs={{0,4},{4,0},{8,12},{12,8},{16,20},{20,16},{24,28},{28,24},{1,5},{5... | collective-permute-start | bytes 7667720 | tf_op jit(solution)/shard_map/ppermute | solution.py:46
  (37 other events, 140.3 us)
where the time goes:
time: 379 us; the launch traced here: 375 us
  Pallas kernels  94 us (25%)
  waiting for transfers between devices  92.6 us (24%)
  starting transfers between devices  85.5 us (23%)
  local copies, waits for them, and re-layouts  45 us (12%)
  other arithmetic  31.9 us (8%)
  matrix products  24.1 us (6%)
    ppermute x18, waiting for transfers between devices, shift(): lax.ppermute(value, axis, [(i, (i + step) % count) for i in range(count)])  46.8 us
    ppermute x17, waiting for transfers between devices, swap(): return lax.ppermute(value, axis, [(i, i ^ bit) for i in range(count)])  37.3 us
    all_to_all x6, starting transfers between devices, exchange(): return lax.all_to_all(value, axis, split_axis=0, concat_axis=0)  37.1 us
    pallas_call x2, Pallas kernels, expert_grads(): pl.pallas_call(expert_grads_kernel, grid_spec=pltpu.PrefetchScalarGridSpe...  30.3 us
    ppermute x18, starting transfers between devices, shift(): lax.ppermute(value, axis, [(i, (i + step) % count) for i in range(count)])  30.1 us
    pallas_call x1, Pallas kernels, expert(): pl.pallas_call(expert_kernel, grid=(hidden // FF_TILE,), in_specs=[pl.Blo...  26.6 us
    dot_general x16, matrix products, dot(): lax.dot_general(left, right, (dims, ((), ())), preferred_element_type=F32)  19 us
    ppermute x17, starting transfers between devices, swap(): return lax.ppermute(value, axis, [(i, i ^ bit) for i in range(count)])  18.2 us
  transfers between devices with their start and end apart: 41, of which 18 were waited for; matrix products, arithmetic and copies ran while one was open for 20% of the time, Pallas kernels for 23%

commit v1 on v0

--- a/solution.py
+++ b/solution.py
@@ -715,7 +715,7 @@
     head_weights = jnp.stack([head_rows(w) for w in (w_query, w_key, w_value)])
 
     own_sent, head_weights = after(
-        (upstream_sent(member, dispatch, cotangent), head_weights), token_parts[2][1]
+        (upstream_sent(member, dispatch, cotangent), head_weights), token_parts[-1][1]
     )
     upstream_slots = to_experts(own_sent)
     sequence = in_order(token_parts, "context")
@@ -825,9 +825,6 @@
         qkv, normed, bias, log_total, exact, grads_in
     )
     weight_grads, out_returns = lax.optimization_barrier((weight_grads, out_returns))
-    cut = down_sent.shape[1] // 2
-    down_first = swap(after(down_sent[:, :cut], up_arrived), "context", quarter)
-    weight_grads, down_first = lax.optimization_barrier((weight_grads, down_first))
     table_part = jnp.dot(diagonals[:, 0, rows:], bucket_match, precision=HIGHEST)
     table_line = lax.dynamic_update_slice(
         jnp.zeros((count * group, buckets), F32), table_part, (here * group, 0)
@@ -846,36 +843,11 @@
         axis=1,
     )
     pack = halve_sum(pack, "expert", bits).astype(BF16)
+    arrived = context_steps(grads_out)
     pack = jnp.concatenate([pack, proj_rows], axis=0)
     pack = in_order(ring_parts(pack[None], "context"), "context")
-    down_second, grads_out = after((down_sent[:, cut:], grads_out), pack)
-    down_second = swap(down_second, "context", quarter)
-    arrived = context_steps(grads_out)
-    up_grad = up_kept.astype(F32) + up_arrived.astype(F32)
-    gated = (spread * gates[:, :, None]).reshape(rows, slots)
-    output = middle + jnp.dot(
-        gated, out_returns.reshape(slots, width).astype(F32), precision=HIGHEST
-    )
-    half = width // 2
-    near = jnp.stack(
-        [
-            double_gather(pack[:, :, :half], "expert", bits[:0:-1]),
-            double_gather(pack[:, :, half:], "expert", bits[1:]),
-        ]
-    )
-    near, arrived, down_second = lax.optimization_barrier((near, arrived, down_second))
-    far = swap(near, "expert", bits[0])
-    down_arrived = jnp.concatenate([down_first, down_second], axis=1)
-    down_grad = down_kept.astype(F32) + down_arrived.astype(F32)
-    up_grad = halve_sum(up_grad, "context", low_bits, BF16)
-    down_grad = halve_sum(down_grad, "context", low_bits, BF16)
-    grad_query, grad_key, grad_value, grad_proj, small, gain_attn_total = assemble(
-        own[None], near, far, w_query, w_key, w_value, bits, chunk
-    )
-    gain_attn_total = gain_attn_total[:, 0] / gain_attn
-    router_total = small[:experts].T
-    gain_moe_total = small[experts]
-    table_total = small[experts + 1, : HEADS * buckets].reshape(HEADS, buckets).T
+    pack, arrived = lax.optimization_barrier((pack, arrived))
+    down_arrived = swap(after(down_sent, pack), "context", quarter)
     normed_grads = 0.0
     for j, weight in enumerate((w_query, w_key, w_value)):
         part = arrived[:, j].reshape(count * held, rows)[:width]
@@ -883,6 +855,35 @@
     attention_scale = lax.rsqrt(jnp.mean(source * source, axis=1, keepdims=True) + EPSILON)
     token_norm_grads, unused = normalize_back(normed_grads, source, attention_scale, gain_attn)
     token_grads = (middle_grads + token_norm_grads).astype(BF16)
+    up_grad = up_kept.astype(F32) + up_arrived.astype(F32)
+    up_grad = halve_sum(up_grad, "context", low_bits, BF16)
+    gated = (spread * gates[:, :, None]).reshape(rows, slots)
+    output = middle + jnp.dot(
+        gated, out_returns.reshape(slots, width).astype(F32), precision=HIGHEST
+    )
+    half = width // 2
+    sides = (bits[:0:-1], bits[1:])
+    parts = [
+        double_gather(part, "expert", order[:1])
+        for part, order in zip((pack[:, :, :half], pack[:, :, half:]), sides)
+    ]
+    parts, token_grads, up_grad, output = lax.optimization_barrier(
+        (parts, token_grads, up_grad, output)
+    )
+    near = jnp.stack(
+        [double_gather(part, "expert", order[1:]) for part, order in zip(parts, sides)]
+    )
+    near, down_arrived = lax.optimization_barrier((near, down_arrived))
+    far = swap(near, "expert", bits[0])
+    down_grad = down_kept.astype(F32) + down_arrived.astype(F32)
+    down_grad = halve_sum(down_grad, "context", low_bits, BF16)
+    grad_query, grad_key, grad_value, grad_proj, small, gain_attn_total = assemble(
+        own[None], near, far, w_query, w_key, w_value, bits, chunk
+    )
+    gain_attn_total = gain_attn_total[:, 0] / gain_attn
+    router_total = small[:experts].T
+    gain_moe_total = small[experts]
+    table_total = small[experts + 1, : HEADS * buckets].reshape(HEADS, buckets).T
     return (
         output.astype(BF16),
         token_grads,

time: 379 us -> 368 us (0.971)
  other arithmetic: 31.9 us -> 26 us
  waiting for transfers between devices: 92.6 us -> 86.8 us
    ppermute x18, waiting for transfers between devices: 46.8 us -> 40.1 us  [shift(): lax.ppermute(value, axis, [(i, (i + step) % count) for i in range(count)])]
    unnamed x93 -> x91, local copies, waits for them, and re-layouts: 10 us -> 7.57 us
    ppermute x17 -> x16, waiting for transfers between devices: 37.3 us -> 38.6 us  [swap(): return lax.ppermute(value, axis, [(i, i ^ bit) for i in range(count)])]
    ppermute x17 -> x16, starting transfers between devices: 18.2 us -> 18.5 us  [swap(): return lax.ppermute(value, axis, [(i, i ^ bit) for i in range(count)])]
  transfers between devices with their start and end apart: 41 -> 40, of which waited for: 18 -> 21; matrix products, arithmetic and copies ran while one was open for 20% -> 20% of each run, Pallas kernels for 23% -> 24%
where the time goes in v1:
time: 368 us; the launch traced here: 365 us
  Pallas kernels  94 us (26%)
  starting transfers between devices  88.3 us (24%)
  waiting for transfers between devices  86.8 us (24%)
  local copies, waits for them, and re-layouts  43 us (12%)
  other arithmetic  26 us (7%)
  matrix products  24.7 us (7%)
    ppermute x18, waiting for transfers between devices, shift(): lax.ppermute(value, axis, [(i, (i + step) % count) for i in range(count)])  40.1 us
    ppermute x16, waiting for transfers between devices, swap(): return lax.ppermute(value, axis, [(i, i ^ bit) for i in range(count)])  38.6 us
    all_to_all x6, starting transfers between devices, exchange(): return lax.all_to_all(value, axis, split_axis=0, concat_axis=0)  37.5 us
    ppermute x18, starting transfers between devices, shift(): lax.ppermute(value, axis, [(i, (i + step) % count) for i in range(count)])  32.3 us
    pallas_call x2, Pallas kernels, expert_grads(): pl.pallas_call(expert_grads_kernel, grid_spec=pltpu.PrefetchScalarGridSpe...  30.3 us
    pallas_call x1, Pallas kernels, expert(): pl.pallas_call(expert_kernel, grid=(hidden // FF_TILE,), in_specs=[pl.Blo...  26.6 us
    dot_general x16, matrix products, dot(): lax.dot_general(left, right, (dims, ((), ())), preferred_element_type=F32)  19.6 us
    ppermute x16, starting transfers between devices, swap(): return lax.ppermute(value, axis, [(i, i ^ bit) for i in range(count)])  18.5 us
  transfers between devices with their start and end apart: 40, of which 21 were waited for; matrix products, arithmetic and copies ran while one was open for 20% of the time, Pallas kernels for 24%

profile of v1, /device:TPU:0, one launch (start us, length us, event | category | flops | bytes accessed | tf_op | source)
XLA Modules:
  0.0 364.7 jit_solution(8240448321004742282)
XLA Ops:
  0.7 3.1 collective-permute-start
  10.3 4.8 %collective-permute-done = bf16[256,768]{1,0:T(8,128)(2,1)S(1)} collective-permute-done((bf16[256,768]{1,0:T(8,128)(2,1)}, bf16[256,768]{1,0:T(8,128)(2,1)S(1)}, u32[]{:S(2)}, u32[]{:S(2)}) %collective-permute-start) | collective-permute-done | bytes 393248 | tf_op jit(solution)/shard_map/ppermute | solution.py:41
  15.1 1.9 convolution_convert_fusion.3
  18.4 8.9 %collective-permute-done.2 = bf16[256,768]{1,0:T(8,128)(2,1)} collective-permute-done((bf16[256,768]{1,0:T(8,128)(2,1)S(1)}, bf16[256,768]{1,0:T(8,128)(2,1)}, u32[]{:S(2)}, u32[]{:S(2)}) %collective-permute-start.2) | collective-permute-done | bytes 393248 | tf_op jit(solution)/shard_map/ppermute | solution.py:41
  27.3 3.6 all-to-all-start
  33.8 8.6 %collective-permute-done.1 = bf16[256,768]{1,0:T(8,128)(2,1)} collective-permute-done((bf16[256,768]{1,0:T(8,128)(2,1)S(1)}, bf16[256,768]{1,0:T(8,128)(2,1)}, u32[]{:S(2)}, u32[]{:S(2)}) %collective-permute-start.1) | collective-permute-done | bytes 393248 | tf_op jit(solution)/shard_map/ppermute | solution.py:41
  49.1 2.9 collective-permute-start.4
  52.0 10.6 %attend.1 = (bf16[1024,768]{1,0:T(8,128)(2,1)}, bf16[3,192,1024]{2,1,0:T(8,128)(2,1)}, bf16[4,192,256]{2,1,0:T(8,128)(2,1)}, f32[3,64,1024]{2,1,0:T(8,128)}, f32[3,1,1024]{2,1,0:T(1,128)}) custom-call(bf16[1024,768]{1,0:T(8,128)(2,1)} %constant_dynamic-update-slice_fusion.16.tokens, f32[1,768]{1,0:T(1,128)} %broadcast_in_dim.126.gain, ...), custom_call_target="tpu_custom_call" | custom-call | flops 2113929216 | bytes 6291456 | tf_op jit(solution)/shard_map/attend/pallas_call | solution.py:314
  62.7 3.3 collective-permute-done.4
  74.0 4.4 %all-to-all-start.1 = ((bf16[8,136,768]{2,1,0:T(8,128)(2,1)}), bf16[8,136,768]{2,1,0:T(8,128)(2,1)}, u32[]{:S(2)}, u32[]{:S(2)}) async-start(bf16[8,136,768]{2,1,0:T(8,128)(2,1)} %fusion.3), calls=%async_computation.1 | async-start | bytes 3342336 | tf_op jit(solution)/shard_map/all_to_all | solution.py:611
  79.2 2.0 collective-permute-start.6
  84.6 2.0 collective-permute-done.6
  90.6 1.9 convolution_convert_fusion.2
  92.5 8.0 %all-to-all-done.1.other_upstream = bf16[8,136,768]{2,1,0:T(8,128)(2,1)} async-done(((bf16[8,136,768]{2,1,0:T(8,128)(2,1)}), bf16[8,136,768]{2,1,0:T(8,128)(2,1)}, u32[]{:S(2)}, u32[]{:S(2)}) %all-to-all-start.1) | async-done | bytes 1671200 | tf_op jit(solution)/shard_map/all_to_all | solution.py:611
  100.6 16.4 %all-to-all-start.2 = ((bf16[8,128,768]{2,1,0:T(8,128)(2,1)}), bf16[8,128,768]{2,1,0:T(8,128)(2,1)S(1)}, u32[]{:S(2)}, u32[]{:S(2)}) async-start(bf16[8,128,768]{2,1,0:T(8,128)(2,1)} %bitcast.180), calls=%async_computation.2 | async-start | bytes 3145728 | tf_op jit(solution)/shard_map/all_to_all | solution.py:611
  118.9 2.9 collective-permute-start.8
  129.2 10.6 %collective-permute-done.8 = bf16[256,768]{1,0:T(8,128)(2,1)} collective-permute-done((bf16[256,768]{1,0:T(8,128)(2,1)S(1)}, bf16[256,768]{1,0:T(8,128)(2,1)}, u32[]{:S(2)}, u32[]{:S(2)}) %collective-permute-start.8) | collective-permute-done | bytes 393248 | tf_op jit(solution)/shard_map/ppermute | solution.py:46
  139.8 3.5 convolution_convert_fusion
  143.3 4.4 %all-to-all-start.3 = ((bf16[8,128,768]{2,1,0:T(8,128)(2,1)}), bf16[8,128,768]{2,1,0:T(8,128)(2,1)}, u32[]{:S(2)}, u32[]{:S(2)}) async-start(bf16[8,128,768]{2,1,0:T(8,128)(2,1)} %bitcast.181), calls=%async_computation.3 | async-start | bytes 3145728 | tf_op jit(solution)/shard_map/all_to_all | solution.py:611
  150.4 26.6 %expert.1 = (bf16[1024,768]{1,0:T(8,128)(2,1)}, bf16[8,136,768]{2,1,0:T(8,128)(2,1)}) custom-call(bf16[1024,768]{1,0:T(8,128)(2,1)} %bitcast.177, bf16[8,136,768]{2,1,0:T(8,128)(2,1)} %copy-done.17, f32[8,1,128]{2,1,0:T(1,128)} %fusion.48.gate.own_gate, bf16[768,3072]{1,0:T(8,128)(2,1)} %bitcast.216, bf16[3072,768]{1,0:T(8,128)(2,1)} %bitcast.219), custom_call_target="tpu_custom_call" | custom-call | flops 24159191040 | bytes 9437184 | tf_op jit(solution)/shard_map/expert/pallas_call | solution.py:386
  176.9 1.9 select_reduce_fusion
  179.7 4.1 %all-to-all-start.4 = ((bf16[8,136,768]{2,1,0:T(8,128)(2,1)}), bf16[8,136,768]{2,1,0:T(8,128)(2,1)S(1)}, u32[]{:S(2)}, u32[]{:S(2)}) async-start(bf16[8,136,768]{2,1,0:T(8,128)(2,1)} %get-tuple-element.89), calls=%async_computation.4 | async-start | bytes 3342336 | tf_op jit(solution)/shard_map/all_to_all | solution.py:611
  184.4 15.0 %expert_grads.2 = (bf16[1,768,768]{2,1,0:T(8,128)(2,1)}, bf16[1,768,768]{2,1,0:T(8,128)(2,1)}) custom-call(s32[1]{0:T(128)} %bitcast.28.index, bf16[1024,768]{1,0:T(8,128)(2,1)} %bitcast.178, bf16[1024,768]{1,0:T(8,128)(2,1)} %bitcast.27.other_rows, bf16[8,136,768]{2,1,0:T(8,128)(2,1)} %copy-done.17, bf16[8,136,768]{2,1,0:T(8,128)(2,1)} %all-to-all-done.1.other_upstream, ...), custom_call_target="tpu_custom_call" | custom-call | flops 9663676416 | bytes 6291456 | tf_op jit(solution)/shard_map/expert_grads/pallas_call | solution.py:423
  199.4 15.4 %expert_grads.3 = (bf16[1,768,768]{2,1,0:T(8,128)(2,1)}, bf16[1,768,768]{2,1,0:T(8,128)(2,1)}) custom-call(s32[1]{0:T(128)} %bitcast.34.index, bf16[1024,768]{1,0:T(8,128)(2,1)} %bitcast.179, bf16[1024,768]{1,0:T(8,128)(2,1)} %bitcast.27.other_rows, bf16[8,136,768]{2,1,0:T(8,128)(2,1)} %copy-done.17, bf16[8,136,768]{2,1,0:T(8,128)(2,1)} %all-to-all-done.1.other_upstream, ...), custom_call_target="tpu_custom_call" | custom-call | flops 9663676416 | bytes 6291456 | tf_op jit(solution)/shard_map/expert_grads/pallas_call | solution.py:423
  215.9 6.5 %token_back.1 = (f32[256,768]{1,0:T(8,128)}, bf16[256,768]{1,0:T(8,128)(2,1)}, bf16[768,256]{1,0:T(8,128)(2,1)}, f32[1,768]{1,0:T(1,128)}, f32[8,768]{1,0:T(8,128)}) custom-call(bf16[8,136,768]{2,1,0:T(8,128)(2,1)} %copy-done.6, bf16[256,1024]{1,0:T(8,128)(2,1)} %get-tuple-element.132.dispatch, f32[256,8]{1,0:T(8,128)} %fusion.37.gates, ...), custom_call_target="tpu_custom_call" | custom-call | tf_op jit(solution)/shard_map/token_back/pallas_call | solution.py:580
  223.5 2.0 collective-permute-start.9
  226.4 3.0 collective-permute-start.11
  235.2 4.5 %all-to-all-start.5 = ((bf16[8,128,768]{2,1,0:T(8,128)(2,1)}), bf16[8,128,768]{2,1,0:T(8,128)(2,1)}, u32[]{:S(2)}, u32[]{:S(2)}) async-start(bf16[8,128,768]{2,1,0:T(8,128)(2,1)} %bitcast.197), calls=%async_computation.5 | async-start | bytes 3145728 | tf_op jit(solution)/shard_map/all_to_all | solution.py:611
  239.7 13.0 %attend_back.1 = (bf16[4,3,192,256]{3,2,1,0:T(8,128)(2,1)}, bf16[3,192,768]{2,1,0:T(8,128)(2,1)}, f32[3,1,1280]{2,1,0:T(1,128)}) custom-call(bf16[3,192,1024]{2,1,0:T(8,128)(2,1)} %get-tuple-element.73.qkv, bf16[1024,768]{1,0:T(8,128)(2,1)} %get-tuple-element.74.normed, f32[3,1,1280]{2,1,0:T(1,128)} %broadcast_in_dim.127.bias, ...), custom_call_target="tpu_custom_call" | custom-call | flops 2717908992 | bytes 6291456 | tf_op jit(solution)/shard_map/attend_back/pallas_call | solution.py:348
  255.3 2.7 collective-permute-start.25
  258.1 3.8 %collective-permute-start.27 = (bf16[1,3,192,256]{3,2,1,0:T(8,128)(2,1)S(1)}, bf16[1,3,192,256]{3,2,1,0:T(8,128)(2,1)}, u32[]{:S(2)}, u32[]{:S(2)}) collective-permute-start(bf16[1,3,192,256]{3,2,1,0:T(8,128)(2,1)S(1)} %get-tuple-element.141), channel_id=1, source_target_pairs={{0,3},{1,0},{2,1},{3,2},{4,7},{5,4},{6,5},{7,6},{8,11},{9,8},{10,9... | collective-permute-start | bytes 884744 | tf_op jit(solution)/shard_map/ppermute | solution.py:41
  263.9 2.0 collective-permute-start.17
  266.0 3.0 add_bitcast_fusion
  268.9 3.6 collective-permute-done.17
  274.5 4.5 %collective-permute-done.25 = bf16[1,3,192,256]{3,2,1,0:T(8,128)(2,1)} collective-permute-done((bf16[1,3,192,256]{3,2,1,0:T(8,128)(2,1)}, bf16[1,3,192,256]{3,2,1,0:T(8,128)(2,1)}, u32[]{:S(2)}, u32[]{:S(2)}) %collective-permute-start.25) | collective-permute-done | bytes 294944 | tf_op jit(solution)/shard_map/ppermute | solution.py:41
  282.6 2.1 collective-permute-start.14
  284.8 5.2 %collective-permute-start.19 = (bf16[1,24,768]{2,1,0:T(8,128)(2,1)S(1)}, bf16[1,24,768]{2,1,0:T(8,128)(2,1)S(1)}, u32[]{:S(2)}, u32[]{:S(2)}) collective-permute-start(bf16[1,24,768]{2,1,0:T(8,128)(2,1)S(1)} %get-tuple-element.159), channel_id=1, source_target_pairs={{0,2},{1,3},{2,0},{3,1},{4,6},{5,7},{6,4},{7,5},{8,10},{9,11},{10,... | collective-permute-start | bytes 110600 | tf_op jit(solution)/shard_map/ppermute | solution.py:41
  291.7 3.8 %collective-permute-start.21 = (bf16[1,24,768]{2,1,0:T(8,128)(2,1)S(1)}, bf16[1,24,768]{2,1,0:T(8,128)(2,1)S(1)}, u32[]{:S(2)}, u32[]{:S(2)}) collective-permute-start(bf16[1,24,768]{2,1,0:T(8,128)(2,1)S(1)} %get-tuple-element.157), channel_id=1, source_target_pairs={{0,3},{1,0},{2,1},{3,2},{4,7},{5,4},{6,5},{7,6},{8,11},{9,8},{10,9... | collective-permute-start | bytes 110600 | tf_op jit(solution)/shard_map/ppermute | solution.py:41
  297.5 3.1 collective-permute-done.15
  300.7 4.3 %fusion.5 = bf16[256,768]{1,0:T(8,128)(2,1)} fusion(f32[256,768]{1,0:T(8,128)S(1)} %copy-done.5, bf16[8,128,768]{2,1,0:T(8,128)(2,1)} %all-to-all-done.5, f32[256,8]{0,1:T(8,128)S(1)} %copy-done.37, s32[256,8]{0,1:T(8,128)S(1)} %copy-done.36, pred[256,8]{0,1:T(8,128)(4,1)S(1)} %fusion.43), kind=kOutput, calls=%fused_computation.22 | convolution fusion | flops 2417623040 | bytes 2770944 | tf_op jit(solution)/shard_map/dot_general | solution.py:861
  305.0 3.8 %collective-permute-start.23 = (bf16[1,104,768]{2,1,0:T(8,128)(2,1)S(1)}, bf16[1,104,768]{2,1,0:T(8,128)(2,1)S(1)}, u32[]{:S(2)}, u32[]{:S(2)}) collective-permute-start(bf16[1,104,768]{2,1,0:T(8,128)(2,1)S(1)} %maximum_bitcast_fusion.2), channel_id=1, source_target_pairs={{0,3},{1,0},{2,1},{3,2},{4,7},{5,4},{6,5},{7,6},{8,11},{9,8},{10,9... | collective-permute-start | bytes 479240 | tf_op jit(solution)/shard_map/ppermute | solution.py:41
  309.2 2.6 collective-permute-done.23
  311.8 6.2 %collective-permute-done.24 = bf16[1,104,768]{2,1,0:T(8,128)(2,1)S(1)} collective-permute-done((bf16[1,104,768]{2,1,0:T(8,128)(2,1)S(1)}, bf16[1,104,768]{2,1,0:T(8,128)(2,1)S(1)}, u32[]{:S(2)}, u32[]{:S(2)}) %collective-permute-start.24) | collective-permute-done | bytes 159776 | tf_op jit(solution)/shard_map/ppermute | solution.py:41
  325.2 2.5 collective-permute-done.29
  327.9 4.6 %collective-permute-done.28 = bf16[4,104,384]{2,1,0:T(8,128)(2,1)S(1)} collective-permute-done((bf16[4,104,384]{2,1,0:T(8,128)(2,1)S(1)}, bf16[4,104,384]{2,1,0:T(8,128)(2,1)S(1)}, u32[]{:S(2)}, u32[]{:S(2)}) %collective-permute-start.28) | collective-permute-done | bytes 319520 | tf_op jit(solution)/shard_map/ppermute | solution.py:46
  335.9 7.1 %collective-permute-done.30 = bf16[2,4,104,384]{3,2,1,0:T(8,128)(2,1)S(1)} collective-permute-done((bf16[2,4,104,384]{3,2,1,0:T(8,128)(2,1)S(1)}, bf16[2,4,104,384]{3,2,1,0:T(8,128)(2,1)S(1)}, u32[]{:S(2)}, u32[]{:S(2)}) %collective-permute-start.30) | collective-permute-done | bytes 639008 | tf_op jit(solution)/shard_map/ppermute | solution.py:46
  348.0 2.2 collective-permute-done.33.far
  351.7 6.9 %assemble.1 = (f32[768,768]{1,0:T(8,128)}, f32[768,768]{1,0:T(8,128)}, f32[768,768]{1,0:T(8,128)}, f32[768,768]{1,0:T(8,128)}, f32[64,768]{1,0:T(8,128)}, /*index=5*/f32[768,1]{1,0:T(8,128)}) custom-call(s32[1]{0:T(128)} %bitcast.65.index, bf16[2,2,2,4,104,384]{5,4,3,2,1,0:T(8,128)(2,1)} %copy-done.2, bf16[2,2,2,4,104,384]{5,4,3,2,1,0:T(8,128)(2,1)} %copy-done.16, ...), custom_call_target="tpu_custom_call" | custom-call | tf_op jit(solution)/shard_map/assemble/pallas_call | solution.py:516
  (261 shorter events, 92.8 us)
Async XLA Ops:
  0.6 45.3 %copy-start = (f32[32,12]{0,1:T(8,128)S(1)}, f32[32,12]{0,1:T(8,128)}, u32[]{:S(2)}) copy-start(f32[32,12]{0,1:T(8,128)} %param.20) | copy-start | bytes 4612
  0.7 14.4 %collective-permute-start = (bf16[256,768]{1,0:T(8,128)(2,1)}, bf16[256,768]{1,0:T(8,128)(2,1)S(1)}, u32[]{:S(2)}, u32[]{:S(2)}) collective-permute-start(bf16[256,768]{1,0:T(8,128)(2,1)} %param.14), channel_id=1, source_target_pairs={{0,1},{1,2},{2,3},{3,0},{4,5},{5,6},{6,7},{7,4},{8,9},{9,10},{10,1... | collective-permute-start | bytes 1179656 | tf_op jit(solution)/shard_map/ppermute | solution.py:41
  15.1 12.2 %collective-permute-start.2 = (bf16[256,768]{1,0:T(8,128)(2,1)S(1)}, bf16[256,768]{1,0:T(8,128)(2,1)}, u32[]{:S(2)}, u32[]{:S(2)}) collective-permute-start(bf16[256,768]{1,0:T(8,128)(2,1)S(1)} %collective-permute-done), channel_id=1, source_target_pairs={{0,1},{1,2},{2,3},{3,0},{4,5},{5,6},{6,7},{7,4},{8,9},{9,10},{10,1... | collective-permute-start | bytes 1179656 | tf_op jit(solution)/shard_map/ppermute | solution.py:41
  27.3 38.7 %all-to-all-start = ((bf16[8,136,768]{2,1,0:T(8,128)(2,1)}), bf16[8,136,768]{2,1,0:T(8,128)(2,1)S(1)}, u32[]{:S(2)}, u32[]{:S(2)}) async-start(bf16[8,136,768]{2,1,0:T(8,128)(2,1)} %fusion.2), calls=%async_computation | async-start | bytes 3342336 | tf_op jit(solution)/shard_map/all_to_all | solution.py:611
  30.9 11.5 %collective-permute-start.1 = (bf16[256,768]{1,0:T(8,128)(2,1)S(1)}, bf16[256,768]{1,0:T(8,128)(2,1)}, u32[]{:S(2)}, u32[]{:S(2)}) collective-permute-start(bf16[256,768]{1,0:T(8,128)(2,1)S(1)} %copy-done.3), channel_id=1, source_target_pairs={{0,3},{1,0},{2,1},{3,2},{4,7},{5,4},{6,5},{7,6},{8,11},{9,8},{10,9... | collective-permute-start | bytes 1179656 | tf_op jit(solution)/shard_map/ppermute | solution.py:41
  33.1 15.5 %copy-start.31 = (f32[768]{0:T(1024)S(1)}, f32[768]{0:T(1024)}, u32[]{:S(2)}) copy-start(f32[768]{0:T(1024)} %param.21) | copy-start | bytes 9220
  33.1 16.1 %copy-start.39 = (s32[256,2]{0,1:T(2,128)S(1)}, s32[256,2]{0,1:T(2,128)}, u32[]{:S(2)}) copy-start(s32[256,2]{0,1:T(2,128)} %param.25) | copy-start | bytes 6148
  46.0 20.0 %collective-permute-start.3 = (bf16[256,768]{1,0:T(8,128)(2,1)}, bf16[256,768]{1,0:T(8,128)(2,1)}, u32[]{:S(2)}, u32[]{:S(2)}) collective-permute-start(bf16[256,768]{1,0:T(8,128)(2,1)} %cotangent.1), channel_id=1, source_target_pairs={{0,2},{1,3},{2,0},{3,1},{4,6},{5,7},{6,4},{7,5},{8,10},{9,11},{10,... | collective-permute-start | bytes 1179656 | tf_op jit(solution)/shard_map/ppermute | solution.py:46
  49.1 16.9 %collective-permute-start.4 = (s32[2,256]{1,0:T(2,128)S(1)}, s32[2,256]{1,0:T(2,128)S(1)}, u32[]{:S(2)}, u32[]{:S(2)}) collective-permute-start(s32[2,256]{1,0:T(2,128)S(1)} %bitcast.214), channel_id=1, source_target_pairs={{0,2},{1,3},{2,0},{3,1},{4,6},{5,7},{6,4},{7,5},{8,10},{9,11},{10,... | collective-permute-start | bytes 6152 | tf_op jit(solution)/shard_map/ppermute | solution.py:46
  69.1 14.0 %collective-permute-start.5 = (bf16[1,192,256]{2,1,0:T(8,128)(2,1)}, bf16[1,192,256]{2,1,0:T(8,128)(2,1)}, u32[]{:S(2)}, u32[]{:S(2)}) collective-permute-start(bf16[1,192,256]{2,1,0:T(8,128)(2,1)} %get-tuple-element.155), channel_id=1, source_target_pairs={{0,2},{1,3},{2,0},{3,1},{4,6},{5,7},{6,4},{7,5},{8,10},{9,11},{10,... | collective-permute-start | bytes 294920 | tf_op jit(solution)/shard_map/ppermute | solution.py:41
  74.0 26.5 %all-to-all-start.1 = ((bf16[8,136,768]{2,1,0:T(8,128)(2,1)}), bf16[8,136,768]{2,1,0:T(8,128)(2,1)}, u32[]{:S(2)}, u32[]{:S(2)}) async-start(bf16[8,136,768]{2,1,0:T(8,128)(2,1)} %fusion.3), calls=%async_computation.1 | async-start | bytes 3342336 | tf_op jit(solution)/shard_map/all_to_all | solution.py:611
  79.2 7.4 %collective-permute-start.6 = (bf16[1,192,256]{2,1,0:T(8,128)(2,1)S(1)}, bf16[1,192,256]{2,1,0:T(8,128)(2,1)S(1)}, u32[]{:S(2)}, u32[]{:S(2)}) collective-permute-start(bf16[1,192,256]{2,1,0:T(8,128)(2,1)S(1)} %copy-done.29), channel_id=1, source_target_pairs={{0,1},{1,2},{2,3},{3,0},{4,5},{5,6},{6,7},{7,4},{8,9},{9,10},{10,1... | collective-permute-start | bytes 294920 | tf_op jit(solution)/shard_map/ppermute | solution.py:41
  81.2 6.9 %collective-permute-start.7 = (bf16[1,192,256]{2,1,0:T(8,128)(2,1)S(1)}, bf16[1,192,256]{2,1,0:T(8,128)(2,1)S(1)}, u32[]{:S(2)}, u32[]{:S(2)}) collective-permute-start(bf16[1,192,256]{2,1,0:T(8,128)(2,1)S(1)} %copy-done.28), channel_id=1, source_target_pairs={{0,3},{1,0},{2,1},{3,2},{4,7},{5,4},{6,5},{7,6},{8,11},{9,8},{10,9... | collective-permute-start | bytes 294920 | tf_op jit(solution)/shard_map/ppermute | solution.py:41
  90.6 31.3 %copy-start.11 = (bf16[256,768]{1,0:T(8,128)(2,1)}, bf16[256,768]{1,0:T(8,128)(2,1)S(1)}, u32[]{:S(2)}) copy-start(bf16[256,768]{1,0:T(8,128)(2,1)S(1)} %multiply_convert_fusion.routed) | copy-start | bytes 1179652
  100.6 16.5 %copy-start.38 = (f32[256]{0:T(256)S(1)}, f32[256]{0:T(256)}, u32[]{:S(2)}) copy-start(f32[256]{0:T(256)} %fusion.21) | copy-start | bytes 3076
  100.6 39.2 %all-to-all-start.2 = ((bf16[8,128,768]{2,1,0:T(8,128)(2,1)}), bf16[8,128,768]{2,1,0:T(8,128)(2,1)S(1)}, u32[]{:S(2)}, u32[]{:S(2)}) async-start(bf16[8,128,768]{2,1,0:T(8,128)(2,1)} %bitcast.180), calls=%async_computation.2 | async-start | bytes 3145728 | tf_op jit(solution)/shard_map/all_to_all | solution.py:611
  118.9 20.9 %collective-permute-start.8 = (bf16[256,768]{1,0:T(8,128)(2,1)S(1)}, bf16[256,768]{1,0:T(8,128)(2,1)}, u32[]{:S(2)}, u32[]{:S(2)}) collective-permute-start(bf16[256,768]{1,0:T(8,128)(2,1)S(1)} %multiply_convert_fusion.routed), channel_id=1, source_target_pairs={{0,2},{1,3},{2,0},{3,1},{4,6},{5,7},{6,4},{7,5},{8,10},{9,11},{10,... | collective-permute-start | bytes 1179656 | tf_op jit(solution)/shard_map/ppermute | solution.py:46
  143.3 33.7 %all-to-all-start.3 = ((bf16[8,128,768]{2,1,0:T(8,128)(2,1)}), bf16[8,128,768]{2,1,0:T(8,128)(2,1)}, u32[]{:S(2)}, u32[]{:S(2)}) async-start(bf16[8,128,768]{2,1,0:T(8,128)(2,1)} %bitcast.181), calls=%async_computation.3 | async-start | bytes 3145728 | tf_op jit(solution)/shard_map/all_to_all | solution.py:611
  179.7 35.1 %all-to-all-start.4 = ((bf16[8,136,768]{2,1,0:T(8,128)(2,1)}), bf16[8,136,768]{2,1,0:T(8,128)(2,1)S(1)}, u32[]{:S(2)}, u32[]{:S(2)}) async-start(bf16[8,136,768]{2,1,0:T(8,128)(2,1)} %get-tuple-element.89), calls=%async_computation.4 | async-start | bytes 3342336 | tf_op jit(solution)/shard_map/all_to_all | solution.py:611
  199.3 35.1 %collective-permute-start.12 = (bf16[1,768,768]{2,1,0:T(8,128)(2,1)}, bf16[1,768,768]{2,1,0:T(8,128)(2,1)}, u32[]{:S(2)}, u32[]{:S(2)}) collective-permute-start(bf16[1,768,768]{2,1,0:T(8,128)(2,1)} %get-tuple-element.99), channel_id=1, source_target_pairs={{0,1},{1,0},{2,3},{3,2},{4,5},{5,4},{6,7},{7,6},{8,9},{9,8},{10,11... | collective-permute-start | bytes 3538952 | tf_op jit(solution)/shard_map/ppermute | solution.py:46
  223.5 10.9 %collective-permute-start.9 = (bf16[1,192,256]{2,1,0:T(8,128)(2,1)S(1)}, bf16[1,192,256]{2,1,0:T(8,128)(2,1)S(1)}, u32[]{:S(2)}, u32[]{:S(2)}) collective-permute-start(bf16[1,192,256]{2,1,0:T(8,128)(2,1)S(1)} %get-tuple-element.151), channel_id=1, source_target_pairs={{0,2},{1,3},{2,0},{3,1},{4,6},{5,7},{6,4},{7,5},{8,10},{9,11},{10,... | collective-permute-start | bytes 294920 | tf_op jit(solution)/shard_map/ppermute | solution.py:41
  225.5 8.8 %collective-permute-start.10 = (bf16[1,192,256]{2,1,0:T(8,128)(2,1)S(1)}, bf16[1,192,256]{2,1,0:T(8,128)(2,1)S(1)}, u32[]{:S(2)}, u32[]{:S(2)}) collective-permute-start(bf16[1,192,256]{2,1,0:T(8,128)(2,1)S(1)} %get-tuple-element.150), channel_id=1, source_target_pairs={{0,1},{1,2},{2,3},{3,0},{4,5},{5,6},{6,7},{7,4},{8,9},{9,10},{10,1... | collective-permute-start | bytes 294920 | tf_op jit(solution)/shard_map/ppermute | solution.py:41
  226.4 8.0 %collective-permute-start.11 = (bf16[1,192,256]{2,1,0:T(8,128)(2,1)S(1)}, bf16[1,192,256]{2,1,0:T(8,128)(2,1)S(1)}, u32[]{:S(2)}, u32[]{:S(2)}) collective-permute-start(bf16[1,192,256]{2,1,0:T(8,128)(2,1)S(1)} %get-tuple-element.149), channel_id=1, source_target_pairs={{0,3},{1,0},{2,1},{3,2},{4,7},{5,4},{6,5},{7,6},{8,11},{9,8},{10,9... | collective-permute-start | bytes 294920 | tf_op jit(solution)/shard_map/ppermute | solution.py:41
  233.2 29.3 %collective-permute-start.16 = (bf16[4,96,768]{2,1,0:T(8,128)(2,1)}, bf16[4,96,768]{2,1,0:T(8,128)(2,1)}, u32[]{:S(2)}, u32[]{:S(2)}) collective-permute-start(bf16[4,96,768]{2,1,0:T(8,128)(2,1)} %dynamic-slice_bitcast_fusion), channel_id=1, source_target_pairs={{0,4},{4,0},{8,12},{12,8},{16,20},{20,16},{24,28},{28,24},{1,5},{5... | collective-permute-start | bytes 1769480 | tf_op jit(solution)/shard_map/ppermute | solution.py:46
  235.2 37.4 %all-to-all-start.5 = ((bf16[8,128,768]{2,1,0:T(8,128)(2,1)}), bf16[8,128,768]{2,1,0:T(8,128)(2,1)}, u32[]{:S(2)}, u32[]{:S(2)}) async-start(bf16[8,128,768]{2,1,0:T(8,128)(2,1)} %bitcast.197), calls=%async_computation.5 | async-start | bytes 3145728 | tf_op jit(solution)/shard_map/all_to_all | solution.py:611
  255.3 23.7 %collective-permute-start.25 = (bf16[1,3,192,256]{3,2,1,0:T(8,128)(2,1)}, bf16[1,3,192,256]{3,2,1,0:T(8,128)(2,1)}, u32[]{:S(2)}, u32[]{:S(2)}) collective-permute-start(bf16[1,3,192,256]{3,2,1,0:T(8,128)(2,1)} %get-tuple-element.143), channel_id=1, source_target_pairs={{0,2},{1,3},{2,0},{3,1},{4,6},{5,7},{6,4},{7,5},{8,10},{9,11},{10,... | collective-permute-start | bytes 884744 | tf_op jit(solution)/shard_map/ppermute | solution.py:41
  258.0 22.6 %collective-permute-start.26 = (bf16[1,3,192,256]{3,2,1,0:T(8,128)(2,1)}, bf16[1,3,192,256]{3,2,1,0:T(8,128)(2,1)}, u32[]{:S(2)}, u32[]{:S(2)}) collective-permute-start(bf16[1,3,192,256]{3,2,1,0:T(8,128)(2,1)} %get-tuple-element.142), channel_id=1, source_target_pairs={{0,1},{1,2},{2,3},{3,0},{4,5},{5,6},{6,7},{7,4},{8,9},{9,10},{10,1... | collective-permute-start | bytes 884744 | tf_op jit(solution)/shard_map/ppermute | solution.py:41
  258.1 31.9 %collective-permute-start.27 = (bf16[1,3,192,256]{3,2,1,0:T(8,128)(2,1)S(1)}, bf16[1,3,192,256]{3,2,1,0:T(8,128)(2,1)}, u32[]{:S(2)}, u32[]{:S(2)}) collective-permute-start(bf16[1,3,192,256]{3,2,1,0:T(8,128)(2,1)S(1)} %get-tuple-element.141), channel_id=1, source_target_pairs={{0,3},{1,0},{2,1},{3,2},{4,7},{5,4},{6,5},{7,6},{8,11},{9,8},{10,9... | collective-permute-start | bytes 884744 | tf_op jit(solution)/shard_map/ppermute | solution.py:41
  263.9 8.6 %collective-permute-start.17 = (bf16[2,96,768]{2,1,0:T(8,128)(2,1)S(1)}, bf16[2,96,768]{2,1,0:T(8,128)(2,1)S(1)}, u32[]{:S(2)}, u32[]{:S(2)}) collective-permute-start(bf16[2,96,768]{2,1,0:T(8,128)(2,1)S(1)} %fusion.32), channel_id=1, source_target_pairs={{0,16},{4,20},{8,24},{12,28},{16,0},{20,4},{24,8},{28,12},{1,17},{... | collective-permute-start | bytes 884744 | tf_op jit(solution)/shard_map/ppermute | solution.py:46
  272.7 9.7 %collective-permute-start.13 = (bf16[4,80,768]{2,1,0:T(8,128)(2,1)S(1)}, bf16[4,80,768]{2,1,0:T(8,128)(2,1)S(1)}, u32[]{:S(2)}, u32[]{:S(2)}) collective-permute-start(bf16[4,80,768]{2,1,0:T(8,128)(2,1)S(1)} %fusion.29), channel_id=1, source_target_pairs={{0,4},{4,0},{8,12},{12,8},{16,20},{20,16},{24,28},{28,24},{1,5},{5... | collective-permute-start | bytes 1474568 | tf_op jit(solution)/shard_map/ppermute | solution.py:46
  272.8 9.6 %collective-permute-start.18 = (bf16[1,96,768]{2,1,0:T(8,128)(2,1)S(1)}, bf16[1,96,768]{2,1,0:T(8,128)(2,1)S(1)}, u32[]{:S(2)}, u32[]{:S(2)}) collective-permute-start(bf16[1,96,768]{2,1,0:T(8,128)(2,1)S(1)} %dynamic-slice_convert_fusion.2), channel_id=1, source_target_pairs={{0,8},{4,12},{8,0},{12,4},{16,24},{20,28},{24,16},{28,20},{1,9},{5... | collective-permute-start | bytes 442376 | tf_op jit(solution)/shard_map/ppermute | solution.py:46
  282.6 12.9 %collective-permute-start.14 = (bf16[2,80,768]{2,1,0:T(8,128)(2,1)S(1)}, bf16[2,80,768]{2,1,0:T(8,128)(2,1)S(1)}, u32[]{:S(2)}, u32[]{:S(2)}) collective-permute-start(bf16[2,80,768]{2,1,0:T(8,128)(2,1)S(1)} %fusion.35), channel_id=1, source_target_pairs={{0,16},{4,20},{8,24},{12,28},{16,0},{20,4},{24,8},{28,12},{1,17},{... | collective-permute-start | bytes 737288 | tf_op jit(solution)/shard_map/ppermute | solution.py:46
  284.7 15.9 %copy-start.5 = (f32[256,768]{1,0:T(8,128)S(1)}, f32[256,768]{1,0:T(8,128)}, u32[]{:S(2)}) copy-start(f32[256,768]{1,0:T(8,128)} %copy-done.4) | copy-start | bytes 2359300
  284.7 15.9 %copy-start.36 = (s32[256,8]{0,1:T(8,128)S(1)}, s32[256,8]{0,1:T(8,128)}, u32[]{:S(2)}) copy-start(s32[256,8]{0,1:T(8,128)} %copy-done.35) | copy-start | bytes 24580
  284.8 15.9 %copy-start.37 = (f32[256,8]{0,1:T(8,128)S(1)}, f32[256,8]{0,1:T(8,128)}, u32[]{:S(2)}) copy-start(f32[256,8]{0,1:T(8,128)} %copy.77) | copy-start | bytes 24580
  284.8 10.7 %collective-permute-start.19 = (bf16[1,24,768]{2,1,0:T(8,128)(2,1)S(1)}, bf16[1,24,768]{2,1,0:T(8,128)(2,1)S(1)}, u32[]{:S(2)}, u32[]{:S(2)}) collective-permute-start(bf16[1,24,768]{2,1,0:T(8,128)(2,1)S(1)} %get-tuple-element.159), channel_id=1, source_target_pairs={{0,2},{1,3},{2,0},{3,1},{4,6},{5,7},{6,4},{7,5},{8,10},{9,11},{10,... | collective-permute-start | bytes 110600 | tf_op jit(solution)/shard_map/ppermute | solution.py:41
  291.7 5.8 %collective-permute-start.20 = (bf16[1,24,768]{2,1,0:T(8,128)(2,1)S(1)}, bf16[1,24,768]{2,1,0:T(8,128)(2,1)S(1)}, u32[]{:S(2)}, u32[]{:S(2)}) collective-permute-start(bf16[1,24,768]{2,1,0:T(8,128)(2,1)S(1)} %get-tuple-element.158), channel_id=1, source_target_pairs={{0,1},{1,2},{2,3},{3,0},{4,5},{5,6},{6,7},{7,4},{8,9},{9,10},{10,1... | collective-permute-start | bytes 110600 | tf_op jit(solution)/shard_map/ppermute | solution.py:41
  291.7 5.8 %collective-permute-start.21 = (bf16[1,24,768]{2,1,0:T(8,128)(2,1)S(1)}, bf16[1,24,768]{2,1,0:T(8,128)(2,1)S(1)}, u32[]{:S(2)}, u32[]{:S(2)}) collective-permute-start(bf16[1,24,768]{2,1,0:T(8,128)(2,1)S(1)} %get-tuple-element.157), channel_id=1, source_target_pairs={{0,3},{1,0},{2,1},{3,2},{4,7},{5,4},{6,5},{7,6},{8,11},{9,8},{10,9... | collective-permute-start | bytes 110600 | tf_op jit(solution)/shard_map/ppermute | solution.py:41
  295.6 4.9 %collective-permute-start.15 = (bf16[1,80,768]{2,1,0:T(8,128)(2,1)S(1)}, bf16[1,80,768]{2,1,0:T(8,128)(2,1)S(1)}, u32[]{:S(2)}, u32[]{:S(2)}) collective-permute-start(bf16[1,80,768]{2,1,0:T(8,128)(2,1)S(1)} %dynamic-slice_convert_fusion.3), channel_id=1, source_target_pairs={{0,8},{4,12},{8,0},{12,4},{16,24},{20,28},{24,16},{28,20},{1,9},{5... | collective-permute-start | bytes 368648 | tf_op jit(solution)/shard_map/ppermute | solution.py:46
  300.6 8.6 %collective-permute-start.22 = (bf16[1,104,768]{2,1,0:T(8,128)(2,1)S(1)}, bf16[1,104,768]{2,1,0:T(8,128)(2,1)S(1)}, u32[]{:S(2)}, u32[]{:S(2)}) collective-permute-start(bf16[1,104,768]{2,1,0:T(8,128)(2,1)S(1)} %maximum_bitcast_fusion.2), channel_id=1, source_target_pairs={{0,1},{1,2},{2,3},{3,0},{4,5},{5,6},{6,7},{7,4},{8,9},{9,10},{10,1... | collective-permute-start | bytes 479240 | tf_op jit(solution)/shard_map/ppermute | solution.py:41
  305.0 6.8 %collective-permute-start.23 = (bf16[1,104,768]{2,1,0:T(8,128)(2,1)S(1)}, bf16[1,104,768]{2,1,0:T(8,128)(2,1)S(1)}, u32[]{:S(2)}, u32[]{:S(2)}) collective-permute-start(bf16[1,104,768]{2,1,0:T(8,128)(2,1)S(1)} %maximum_bitcast_fusion.2), channel_id=1, source_target_pairs={{0,3},{1,0},{2,1},{3,2},{4,7},{5,4},{6,5},{7,6},{8,11},{9,8},{10,9... | collective-permute-start | bytes 479240 | tf_op jit(solution)/shard_map/ppermute | solution.py:41
  309.2 8.8 %collective-permute-start.24 = (bf16[1,104,768]{2,1,0:T(8,128)(2,1)S(1)}, bf16[1,104,768]{2,1,0:T(8,128)(2,1)S(1)}, u32[]{:S(2)}, u32[]{:S(2)}) collective-permute-start(bf16[1,104,768]{2,1,0:T(8,128)(2,1)S(1)} %collective-permute-done.22), channel_id=1, source_target_pairs={{0,1},{1,2},{2,3},{3,0},{4,5},{5,6},{6,7},{7,4},{8,9},{9,10},{10,1... | collective-permute-start | bytes 479240 | tf_op jit(solution)/shard_map/ppermute | solution.py:41
  318.1 27.2 %collective-permute-start.32 = (bf16[1,768,768]{2,1,0:T(8,128)(2,1)S(1)}, bf16[1,768,768]{2,1,0:T(8,128)(2,1)S(1)}, u32[]{:S(2)}, u32[]{:S(2)}) collective-permute-start(bf16[1,768,768]{2,1,0:T(8,128)(2,1)S(1)} %copy-done.40), channel_id=1, source_target_pairs={{0,1},{1,0},{2,3},{3,2},{4,5},{5,4},{6,7},{7,6},{8,9},{9,8},{10,11... | collective-permute-start | bytes 3538952 | tf_op jit(solution)/shard_map/ppermute | solution.py:46
  320.0 7.8 %collective-permute-start.29 = (bf16[4,104,384]{2,1,0:T(8,128)(2,1)S(1)}, bf16[4,104,384]{2,1,0:T(8,128)(2,1)S(1)}, u32[]{:S(2)}, u32[]{:S(2)}) collective-permute-start(bf16[4,104,384]{2,1,0:T(8,128)(2,1)S(1)} %get-tuple-element.147), channel_id=1, source_target_pairs={{0,16},{4,20},{8,24},{12,28},{16,0},{20,4},{24,8},{28,12},{1,17},{... | collective-permute-start | bytes 958472 | tf_op jit(solution)/shard_map/ppermute | solution.py:46
  322.7 9.8 %collective-permute-start.28 = (bf16[4,104,384]{2,1,0:T(8,128)(2,1)S(1)}, bf16[4,104,384]{2,1,0:T(8,128)(2,1)S(1)}, u32[]{:S(2)}, u32[]{:S(2)}) collective-permute-start(bf16[4,104,384]{2,1,0:T(8,128)(2,1)S(1)} %get-tuple-element.148), channel_id=1, source_target_pairs={{0,8},{4,12},{8,0},{12,4},{16,24},{20,28},{24,16},{28,20},{1,9},{5... | collective-permute-start | bytes 958472 | tf_op jit(solution)/shard_map/ppermute | solution.py:46
  332.5 10.5 %collective-permute-start.30 = (bf16[2,4,104,384]{3,2,1,0:T(8,128)(2,1)S(1)}, bf16[2,4,104,384]{3,2,1,0:T(8,128)(2,1)S(1)}, u32[]{:S(2)}, u32[]{:S(2)}) collective-permute-start(bf16[2,4,104,384]{3,2,1,0:T(8,128)(2,1)S(1)} %pad_maximum_fusion.2), channel_id=1, source_target_pairs={{0,16},{4,20},{8,24},{12,28},{16,0},{20,4},{24,8},{28,12},{1,17},{... | collective-permute-start | bytes 1916936 | tf_op jit(solution)/shard_map/ppermute | solution.py:46
  334.4 10.4 %collective-permute-start.31 = (bf16[2,4,104,384]{3,2,1,0:T(8,128)(2,1)S(1)}, bf16[2,4,104,384]{3,2,1,0:T(8,128)(2,1)S(1)}, u32[]{:S(2)}, u32[]{:S(2)}) collective-permute-start(bf16[2,4,104,384]{3,2,1,0:T(8,128)(2,1)S(1)} %pad_maximum_fusion.3), channel_id=1, source_target_pairs={{0,8},{4,12},{8,0},{12,4},{16,24},{20,28},{24,16},{28,20},{1,9},{5... | collective-permute-start | bytes 1916936 | tf_op jit(solution)/shard_map/ppermute | solution.py:46
  345.3 4.9 %collective-permute-start.33 = (bf16[2,2,2,4,104,384]{5,4,3,2,1,0:T(8,128)(2,1)S(1)}, bf16[2,2,2,4,104,384]{5,4,3,2,1,0:T(8,128)(2,1)S(1)}, u32[]{:S(2)}, u32[]{:S(2)}) collective-permute-start(bf16[2,2,2,4,104,384]{5,4,3,2,1,0:T(8,128)(2,1)S(1)} %pad_maximum_fusion.near), channel_id=1, source_target_pairs={{0,4},{4,0},{8,12},{12,8},{16,20},{20,16},{24,28},{28,24},{1,5},{5... | collective-permute-start | bytes 7667720 | tf_op jit(solution)/shard_map/ppermute | solution.py:46
  (35 other events, 181.4 us)

commit v2 on v1

--- a/solution.py
+++ b/solution.py
@@ -855,7 +855,7 @@
     attention_scale = lax.rsqrt(jnp.mean(source * source, axis=1, keepdims=True) + EPSILON)
     token_norm_grads, unused = normalize_back(normed_grads, source, attention_scale, gain_attn)
     token_grads = (middle_grads + token_norm_grads).astype(BF16)
-    up_grad = up_kept.astype(F32) + up_arrived.astype(F32)
+    up_grad = after(up_kept, pack).astype(F32) + up_arrived.astype(F32)
     up_grad = halve_sum(up_grad, "context", low_bits, BF16)
     gated = (spread * gates[:, :, None]).reshape(rows, slots)
     output = middle + jnp.dot(

time: 368 us -> 371 us (level)
  other arithmetic: 26 us -> 30.8 us
    unnamed x91 -> x97, local copies, waits for them, and re-layouts: 7.57 us -> 8.86 us
  transfers between devices with their start and end apart: 40 -> 40, of which waited for: 21 -> 18; matrix products, arithmetic and copies ran while one was open for 20% -> 21% of each run, Pallas kernels for 24% -> 24%
where the time goes in v2:
time: 371 us; the launch traced here: 367 us
  Pallas kernels  94.1 us (25%)
  starting transfers between devices  86.6 us (23%)
  waiting for transfers between devices  83.1 us (22%)
  local copies, waits for them, and re-layouts  45.7 us (12%)
  other arithmetic  30.8 us (8%)
  matrix products  24.6 us (7%)
    ppermute x18, waiting for transfers between devices, shift(): lax.ppermute(value, axis, [(i, (i + step) % count) for i in range(count)])  40.1 us
    all_to_all x6, starting transfers between devices, exchange(): return lax.all_to_all(value, axis, split_axis=0, concat_axis=0)  37.5 us
    ppermute x16, waiting for transfers between devices, swap(): return lax.ppermute(value, axis, [(i, i ^ bit) for i in range(count)])  35.3 us
    ppermute x18, starting transfers between devices, shift(): lax.ppermute(value, axis, [(i, (i + step) % count) for i in range(count)])  30.7 us
    pallas_call x2, Pallas kernels, expert_grads(): pl.pallas_call(expert_grads_kernel, grid_spec=pltpu.PrefetchScalarGridSpe...  30.4 us
    pallas_call x1, Pallas kernels, expert(): pl.pallas_call(expert_kernel, grid=(hidden // FF_TILE,), in_specs=[pl.Blo...  26.6 us
    dot_general x16, matrix products, dot(): lax.dot_general(left, right, (dims, ((), ())), preferred_element_type=F32)  19.5 us
    ppermute x16, starting transfers between devices, swap(): return lax.ppermute(value, axis, [(i, i ^ bit) for i in range(count)])  18.4 us
  transfers between devices with their start and end apart: 40, of which 18 were waited for; matrix products, arithmetic and copies ran while one was open for 21% of the time, Pallas kernels for 24%

profile of v2, /device:TPU:0, one launch (start us, length us, event | category | flops | bytes accessed | tf_op | source)
XLA Modules:
  0.0 366.7 jit_solution(15275577711262024847)
XLA Ops:
  0.7 3.1 collective-permute-start
  10.3 4.8 %collective-permute-done = bf16[256,768]{1,0:T(8,128)(2,1)S(1)} collective-permute-done((bf16[256,768]{1,0:T(8,128)(2,1)}, bf16[256,768]{1,0:T(8,128)(2,1)S(1)}, u32[]{:S(2)}, u32[]{:S(2)}) %collective-permute-start) | collective-permute-done | bytes 393248 | tf_op jit(solution)/shard_map/ppermute | solution.py:41
  15.1 1.9 convolution_convert_fusion.3
  18.4 8.9 %collective-permute-done.2 = bf16[256,768]{1,0:T(8,128)(2,1)} collective-permute-done((bf16[256,768]{1,0:T(8,128)(2,1)S(1)}, bf16[256,768]{1,0:T(8,128)(2,1)}, u32[]{:S(2)}, u32[]{:S(2)}) %collective-permute-start.2) | collective-permute-done | bytes 393248 | tf_op jit(solution)/shard_map/ppermute | solution.py:41
  27.3 3.6 all-to-all-start
  33.8 8.6 %collective-permute-done.1 = bf16[256,768]{1,0:T(8,128)(2,1)} collective-permute-done((bf16[256,768]{1,0:T(8,128)(2,1)S(1)}, bf16[256,768]{1,0:T(8,128)(2,1)}, u32[]{:S(2)}, u32[]{:S(2)}) %collective-permute-start.1) | collective-permute-done | bytes 393248 | tf_op jit(solution)/shard_map/ppermute | solution.py:41
  42.4 1.8 constant_dynamic-update-slice_fusion.17
  44.2 1.8 constant_dynamic-update-slice_fusion.16.tokens
  49.1 2.9 collective-permute-start.4
  52.0 10.6 %attend.1 = (bf16[1024,768]{1,0:T(8,128)(2,1)}, bf16[3,192,1024]{2,1,0:T(8,128)(2,1)}, bf16[4,192,256]{2,1,0:T(8,128)(2,1)}, f32[3,64,1024]{2,1,0:T(8,128)}, f32[3,1,1024]{2,1,0:T(1,128)}) custom-call(bf16[1024,768]{1,0:T(8,128)(2,1)} %constant_dynamic-update-slice_fusion.16.tokens, f32[1,768]{1,0:T(1,128)} %broadcast_in_dim.126.gain, ...), custom_call_target="tpu_custom_call" | custom-call | flops 2113929216 | bytes 6291456 | tf_op jit(solution)/shard_map/attend/pallas_call | solution.py:314
  62.7 3.3 collective-permute-done.4
  71.0 1.8 convolution_convert_fusion.1
  74.1 4.4 %all-to-all-start.1 = ((bf16[8,136,768]{2,1,0:T(8,128)(2,1)}), bf16[8,136,768]{2,1,0:T(8,128)(2,1)}, u32[]{:S(2)}, u32[]{:S(2)}) async-start(bf16[8,136,768]{2,1,0:T(8,128)(2,1)} %fusion.3), calls=%async_computation.1 | async-start | bytes 3342336 | tf_op jit(solution)/shard_map/all_to_all | solution.py:611
  79.2 2.0 collective-permute-start.6
  81.2 1.8 collective-permute-start.7
  83.1 3.8 %collective-permute-done.6 = bf16[1,192,256]{2,1,0:T(8,128)(2,1)S(1)} collective-permute-done((bf16[1,192,256]{2,1,0:T(8,128)(2,1)}, bf16[1,192,256]{2,1,0:T(8,128)(2,1)S(1)}, u32[]{:S(2)}, u32[]{:S(2)}) %collective-permute-start.6) | collective-permute-done | bytes 98336 | tf_op jit(solution)/shard_map/ppermute | solution.py:41
  90.9 2.0 convolution_convert_fusion.2
  92.9 7.7 %all-to-all-done.1.other_upstream = bf16[8,136,768]{2,1,0:T(8,128)(2,1)} async-done(((bf16[8,136,768]{2,1,0:T(8,128)(2,1)}), bf16[8,136,768]{2,1,0:T(8,128)(2,1)}, u32[]{:S(2)}, u32[]{:S(2)}) %all-to-all-start.1) | async-done | bytes 1671200 | tf_op jit(solution)/shard_map/all_to_all | solution.py:611
  100.6 16.4 %all-to-all-start.2 = ((bf16[8,128,768]{2,1,0:T(8,128)(2,1)}), bf16[8,128,768]{2,1,0:T(8,128)(2,1)S(1)}, u32[]{:S(2)}, u32[]{:S(2)}) async-start(bf16[8,128,768]{2,1,0:T(8,128)(2,1)} %bitcast.180), calls=%async_computation.2 | async-start | bytes 3145728 | tf_op jit(solution)/shard_map/all_to_all | solution.py:611
  118.9 2.9 collective-permute-start.8
  129.2 10.6 %collective-permute-done.8 = bf16[256,768]{1,0:T(8,128)(2,1)} collective-permute-done((bf16[256,768]{1,0:T(8,128)(2,1)S(1)}, bf16[256,768]{1,0:T(8,128)(2,1)}, u32[]{:S(2)}, u32[]{:S(2)}) %collective-permute-start.8) | collective-permute-done | bytes 393248 | tf_op jit(solution)/shard_map/ppermute | solution.py:46
  139.8 3.5 convolution_convert_fusion
  143.3 4.4 %all-to-all-start.3 = ((bf16[8,128,768]{2,1,0:T(8,128)(2,1)}), bf16[8,128,768]{2,1,0:T(8,128)(2,1)}, u32[]{:S(2)}, u32[]{:S(2)}) async-start(bf16[8,128,768]{2,1,0:T(8,128)(2,1)} %bitcast.181), calls=%async_computation.3 | async-start | bytes 3145728 | tf_op jit(solution)/shard_map/all_to_all | solution.py:611
  150.4 26.6 %expert.1 = (bf16[1024,768]{1,0:T(8,128)(2,1)}, bf16[8,136,768]{2,1,0:T(8,128)(2,1)}) custom-call(bf16[1024,768]{1,0:T(8,128)(2,1)} %bitcast.177, bf16[8,136,768]{2,1,0:T(8,128)(2,1)} %copy-done.21, f32[8,1,128]{2,1,0:T(1,128)} %fusion.48.gate.own_gate, bf16[768,3072]{1,0:T(8,128)(2,1)} %bitcast.216, bf16[3072,768]{1,0:T(8,128)(2,1)} %bitcast.219), custom_call_target="tpu_custom_call" | custom-call | flops 24159191040 | bytes 9437184 | tf_op jit(solution)/shard_map/expert/pallas_call | solution.py:386
  177.0 1.9 select_reduce_fusion
  179.7 4.1 %all-to-all-start.4 = ((bf16[8,136,768]{2,1,0:T(8,128)(2,1)}), bf16[8,136,768]{2,1,0:T(8,128)(2,1)S(1)}, u32[]{:S(2)}, u32[]{:S(2)}) async-start(bf16[8,136,768]{2,1,0:T(8,128)(2,1)} %get-tuple-element.90), calls=%async_computation.4 | async-start | bytes 3342336 | tf_op jit(solution)/shard_map/all_to_all | solution.py:611
  184.4 15.0 %expert_grads.2 = (bf16[1,768,768]{2,1,0:T(8,128)(2,1)}, bf16[1,768,768]{2,1,0:T(8,128)(2,1)}) custom-call(s32[1]{0:T(128)} %bitcast.28.index, bf16[1024,768]{1,0:T(8,128)(2,1)} %bitcast.178, bf16[1024,768]{1,0:T(8,128)(2,1)} %bitcast.27.other_rows, bf16[8,136,768]{2,1,0:T(8,128)(2,1)} %copy-done.21, bf16[8,136,768]{2,1,0:T(8,128)(2,1)} %all-to-all-done.1.other_upstream, ...), custom_call_target="tpu_custom_call" | custom-call | flops 9663676416 | bytes 6291456 | tf_op jit(solution)/shard_map/expert_grads/pallas_call | solution.py:423
  199.4 15.4 %expert_grads.3 = (bf16[1,768,768]{2,1,0:T(8,128)(2,1)}, bf16[1,768,768]{2,1,0:T(8,128)(2,1)}) custom-call(s32[1]{0:T(128)} %bitcast.34.index, bf16[1024,768]{1,0:T(8,128)(2,1)} %bitcast.179, bf16[1024,768]{1,0:T(8,128)(2,1)} %bitcast.27.other_rows, bf16[8,136,768]{2,1,0:T(8,128)(2,1)} %copy-done.21, bf16[8,136,768]{2,1,0:T(8,128)(2,1)} %all-to-all-done.1.other_upstream, ...), custom_call_target="tpu_custom_call" | custom-call | flops 9663676416 | bytes 6291456 | tf_op jit(solution)/shard_map/expert_grads/pallas_call | solution.py:423
  215.9 6.5 %token_back.1 = (f32[256,768]{1,0:T(8,128)}, bf16[256,768]{1,0:T(8,128)(2,1)}, bf16[768,256]{1,0:T(8,128)(2,1)}, f32[1,768]{1,0:T(1,128)}, f32[8,768]{1,0:T(8,128)}) custom-call(bf16[8,136,768]{2,1,0:T(8,128)(2,1)} %copy-done.6, bf16[256,1024]{1,0:T(8,128)(2,1)} %get-tuple-element.134.dispatch, f32[256,8]{1,0:T(8,128)} %fusion.37.gates, ...), custom_call_target="tpu_custom_call" | custom-call | tf_op jit(solution)/shard_map/token_back/pallas_call | solution.py:580
  224.2 2.0 collective-permute-start.9
  227.1 3.0 collective-permute-start.11
  235.1 4.5 %all-to-all-start.5 = ((bf16[8,128,768]{2,1,0:T(8,128)(2,1)}), bf16[8,128,768]{2,1,0:T(8,128)(2,1)}, u32[]{:S(2)}, u32[]{:S(2)}) async-start(bf16[8,128,768]{2,1,0:T(8,128)(2,1)} %bitcast.197), calls=%async_computation.5 | async-start | bytes 3145728 | tf_op jit(solution)/shard_map/all_to_all | solution.py:611
  242.4 13.0 %attend_back.1 = (bf16[4,3,192,256]{3,2,1,0:T(8,128)(2,1)}, bf16[3,192,768]{2,1,0:T(8,128)(2,1)}, f32[3,1,1280]{2,1,0:T(1,128)}) custom-call(bf16[3,192,1024]{2,1,0:T(8,128)(2,1)} %get-tuple-element.74.qkv, bf16[1024,768]{1,0:T(8,128)(2,1)} %get-tuple-element.75.normed, f32[3,1,1280]{2,1,0:T(1,128)} %broadcast_in_dim.127.bias, ...), custom_call_target="tpu_custom_call" | custom-call | flops 2717908992 | bytes 6291456 | tf_op jit(solution)/shard_map/attend_back/pallas_call | solution.py:348
  257.7 2.4 collective-permute-start.26
  263.8 2.0 collective-permute-start.17
  266.5 6.2 %collective-permute-done.17 = bf16[2,96,768]{2,1,0:T(8,128)(2,1)S(1)} collective-permute-done((bf16[2,96,768]{2,1,0:T(8,128)(2,1)S(1)}, bf16[2,96,768]{2,1,0:T(8,128)(2,1)S(1)}, u32[]{:S(2)}, u32[]{:S(2)}) %collective-permute-start.17) | collective-permute-done | bytes 294944 | tf_op jit(solution)/shard_map/ppermute | solution.py:46
  277.0 3.2 collective-permute-done.25
  285.5 6.2 %collective-permute-start.19 = (bf16[1,24,768]{2,1,0:T(8,128)(2,1)S(1)}, bf16[1,24,768]{2,1,0:T(8,128)(2,1)S(1)}, u32[]{:S(2)}, u32[]{:S(2)}) collective-permute-start(bf16[1,24,768]{2,1,0:T(8,128)(2,1)S(1)} %get-tuple-element.161), channel_id=1, source_target_pairs={{0,2},{1,3},{2,0},{3,1},{4,6},{5,7},{6,4},{7,5},{8,10},{9,11},{10,... | collective-permute-start | bytes 110600 | tf_op jit(solution)/shard_map/ppermute | solution.py:41
  292.8 3.8 %collective-permute-start.21 = (bf16[1,24,768]{2,1,0:T(8,128)(2,1)S(1)}, bf16[1,24,768]{2,1,0:T(8,128)(2,1)S(1)}, u32[]{:S(2)}, u32[]{:S(2)}) collective-permute-start(bf16[1,24,768]{2,1,0:T(8,128)(2,1)S(1)} %get-tuple-element.159), channel_id=1, source_target_pairs={{0,3},{1,0},{2,1},{3,2},{4,7},{5,4},{6,5},{7,6},{8,11},{9,8},{10,9... | collective-permute-start | bytes 110600 | tf_op jit(solution)/shard_map/ppermute | solution.py:41
  305.9 4.3 %fusion.5 = bf16[256,768]{1,0:T(8,128)(2,1)} fusion(f32[256,768]{1,0:T(8,128)S(1)} %copy-done.5, bf16[8,128,768]{2,1,0:T(8,128)(2,1)} %all-to-all-done.5, f32[256,8]{0,1:T(8,128)} %copy.77, s32[256,8]{0,1:T(8,128)S(1)} %copy-done.40, pred[256,8]{0,1:T(8,128)(4,1)S(1)} %fusion.43), kind=kOutput, calls=%fused_computation.22 | convolution fusion | flops 2417623040 | bytes 2770944 | tf_op jit(solution)/shard_map/dot_general | solution.py:861
  310.2 3.8 %collective-permute-start.23 = (bf16[1,104,768]{2,1,0:T(8,128)(2,1)S(1)}, bf16[1,104,768]{2,1,0:T(8,128)(2,1)S(1)}, u32[]{:S(2)}, u32[]{:S(2)}) collective-permute-start(bf16[1,104,768]{2,1,0:T(8,128)(2,1)S(1)} %maximum_bitcast_fusion.2), channel_id=1, source_target_pairs={{0,3},{1,0},{2,1},{3,2},{4,7},{5,4},{6,5},{7,6},{8,11},{9,8},{10,9... | collective-permute-start | bytes 479240 | tf_op jit(solution)/shard_map/ppermute | solution.py:41
  314.2 2.6 collective-permute-done.23
  316.8 6.0 %collective-permute-done.24 = bf16[1,104,768]{2,1,0:T(8,128)(2,1)S(1)} collective-permute-done((bf16[1,104,768]{2,1,0:T(8,128)(2,1)S(1)}, bf16[1,104,768]{2,1,0:T(8,128)(2,1)S(1)}, u32[]{:S(2)}, u32[]{:S(2)}) %collective-permute-start.24) | collective-permute-done | bytes 159776 | tf_op jit(solution)/shard_map/ppermute | solution.py:41
  325.7 3.0 add_bitcast_fusion
  333.8 1.8 collective-permute-start.31
  335.6 8.7 %collective-permute-done.30 = bf16[2,4,104,384]{3,2,1,0:T(8,128)(2,1)S(1)} collective-permute-done((bf16[2,4,104,384]{3,2,1,0:T(8,128)(2,1)S(1)}, bf16[2,4,104,384]{3,2,1,0:T(8,128)(2,1)S(1)}, u32[]{:S(2)}, u32[]{:S(2)}) %collective-permute-start.30) | collective-permute-done | bytes 639008 | tf_op jit(solution)/shard_map/ppermute | solution.py:46
  349.2 3.1 collective-permute-done.33.far
  353.7 6.9 %assemble.1 = (f32[768,768]{1,0:T(8,128)}, f32[768,768]{1,0:T(8,128)}, f32[768,768]{1,0:T(8,128)}, f32[768,768]{1,0:T(8,128)}, f32[64,768]{1,0:T(8,128)}, /*index=5*/f32[768,1]{1,0:T(8,128)}) custom-call(s32[1]{0:T(128)} %bitcast.65.index, bf16[2,2,2,4,104,384]{5,4,3,2,1,0:T(8,128)(2,1)} %copy-done.2, bf16[2,2,2,4,104,384]{5,4,3,2,1,0:T(8,128)(2,1)} %copy-done.20, ...), custom_call_target="tpu_custom_call" | custom-call | tf_op jit(solution)/shard_map/assemble/pallas_call | solution.py:516
  (267 shorter events, 96.1 us)
Async XLA Ops:
  0.6 45.3 %copy-start = (f32[32,12]{0,1:T(8,128)S(1)}, f32[32,12]{0,1:T(8,128)}, u32[]{:S(2)}) copy-start(f32[32,12]{0,1:T(8,128)} %param.20) | copy-start | bytes 4612
  0.7 14.4 %collective-permute-start = (bf16[256,768]{1,0:T(8,128)(2,1)}, bf16[256,768]{1,0:T(8,128)(2,1)S(1)}, u32[]{:S(2)}, u32[]{:S(2)}) collective-permute-start(bf16[256,768]{1,0:T(8,128)(2,1)} %param.14), channel_id=1, source_target_pairs={{0,1},{1,2},{2,3},{3,0},{4,5},{5,6},{6,7},{7,4},{8,9},{9,10},{10,1... | collective-permute-start | bytes 1179656 | tf_op jit(solution)/shard_map/ppermute | solution.py:41
  15.1 12.2 %collective-permute-start.2 = (bf16[256,768]{1,0:T(8,128)(2,1)S(1)}, bf16[256,768]{1,0:T(8,128)(2,1)}, u32[]{:S(2)}, u32[]{:S(2)}) collective-permute-start(bf16[256,768]{1,0:T(8,128)(2,1)S(1)} %collective-permute-done), channel_id=1, source_target_pairs={{0,1},{1,2},{2,3},{3,0},{4,5},{5,6},{6,7},{7,4},{8,9},{9,10},{10,1... | collective-permute-start | bytes 1179656 | tf_op jit(solution)/shard_map/ppermute | solution.py:41
  27.3 38.7 %all-to-all-start = ((bf16[8,136,768]{2,1,0:T(8,128)(2,1)}), bf16[8,136,768]{2,1,0:T(8,128)(2,1)S(1)}, u32[]{:S(2)}, u32[]{:S(2)}) async-start(bf16[8,136,768]{2,1,0:T(8,128)(2,1)} %fusion.2), calls=%async_computation | async-start | bytes 3342336 | tf_op jit(solution)/shard_map/all_to_all | solution.py:611
  30.9 11.5 %collective-permute-start.1 = (bf16[256,768]{1,0:T(8,128)(2,1)S(1)}, bf16[256,768]{1,0:T(8,128)(2,1)}, u32[]{:S(2)}, u32[]{:S(2)}) collective-permute-start(bf16[256,768]{1,0:T(8,128)(2,1)S(1)} %copy-done.3), channel_id=1, source_target_pairs={{0,3},{1,0},{2,1},{3,2},{4,7},{5,4},{6,5},{7,6},{8,11},{9,8},{10,9... | collective-permute-start | bytes 1179656 | tf_op jit(solution)/shard_map/ppermute | solution.py:41
  33.1 15.5 %copy-start.35 = (f32[768]{0:T(1024)S(1)}, f32[768]{0:T(1024)}, u32[]{:S(2)}) copy-start(f32[768]{0:T(1024)} %param.21) | copy-start | bytes 9220
  33.1 16.1 %copy-start.42 = (s32[256,2]{0,1:T(2,128)S(1)}, s32[256,2]{0,1:T(2,128)}, u32[]{:S(2)}) copy-start(s32[256,2]{0,1:T(2,128)} %param.25) | copy-start | bytes 6148
  46.0 20.0 %collective-permute-start.3 = (bf16[256,768]{1,0:T(8,128)(2,1)}, bf16[256,768]{1,0:T(8,128)(2,1)}, u32[]{:S(2)}, u32[]{:S(2)}) collective-permute-start(bf16[256,768]{1,0:T(8,128)(2,1)} %cotangent.1), channel_id=1, source_target_pairs={{0,2},{1,3},{2,0},{3,1},{4,6},{5,7},{6,4},{7,5},{8,10},{9,11},{10,... | collective-permute-start | bytes 1179656 | tf_op jit(solution)/shard_map/ppermute | solution.py:46
  49.1 16.9 %collective-permute-start.4 = (s32[2,256]{1,0:T(2,128)S(1)}, s32[2,256]{1,0:T(2,128)S(1)}, u32[]{:S(2)}, u32[]{:S(2)}) collective-permute-start(s32[2,256]{1,0:T(2,128)S(1)} %bitcast.214), channel_id=1, source_target_pairs={{0,2},{1,3},{2,0},{3,1},{4,6},{5,7},{6,4},{7,5},{8,10},{9,11},{10,... | collective-permute-start | bytes 6152 | tf_op jit(solution)/shard_map/ppermute | solution.py:46
  69.1 13.9 %collective-permute-start.5 = (bf16[1,192,256]{2,1,0:T(8,128)(2,1)}, bf16[1,192,256]{2,1,0:T(8,128)(2,1)S(1)}, u32[]{:S(2)}, u32[]{:S(2)}) collective-permute-start(bf16[1,192,256]{2,1,0:T(8,128)(2,1)} %get-tuple-element.157), channel_id=1, source_target_pairs={{0,2},{1,3},{2,0},{3,1},{4,6},{5,7},{6,4},{7,5},{8,10},{9,11},{10,... | collective-permute-start | bytes 294920 | tf_op jit(solution)/shard_map/ppermute | solution.py:41
  74.1 26.5 %all-to-all-start.1 = ((bf16[8,136,768]{2,1,0:T(8,128)(2,1)}), bf16[8,136,768]{2,1,0:T(8,128)(2,1)}, u32[]{:S(2)}, u32[]{:S(2)}) async-start(bf16[8,136,768]{2,1,0:T(8,128)(2,1)} %fusion.3), calls=%async_computation.1 | async-start | bytes 3342336 | tf_op jit(solution)/shard_map/all_to_all | solution.py:611
  79.2 7.6 %collective-permute-start.6 = (bf16[1,192,256]{2,1,0:T(8,128)(2,1)}, bf16[1,192,256]{2,1,0:T(8,128)(2,1)S(1)}, u32[]{:S(2)}, u32[]{:S(2)}) collective-permute-start(bf16[1,192,256]{2,1,0:T(8,128)(2,1)} %get-tuple-element.156), channel_id=1, source_target_pairs={{0,1},{1,2},{2,3},{3,0},{4,5},{5,6},{6,7},{7,4},{8,9},{9,10},{10,1... | collective-permute-start | bytes 294920 | tf_op jit(solution)/shard_map/ppermute | solution.py:41
  81.2 7.1 %collective-permute-start.7 = (bf16[1,192,256]{2,1,0:T(8,128)(2,1)}, bf16[1,192,256]{2,1,0:T(8,128)(2,1)S(1)}, u32[]{:S(2)}, u32[]{:S(2)}) collective-permute-start(bf16[1,192,256]{2,1,0:T(8,128)(2,1)} %get-tuple-element.155), channel_id=1, source_target_pairs={{0,3},{1,0},{2,1},{3,2},{4,7},{5,4},{6,5},{7,6},{8,11},{9,8},{10,9... | collective-permute-start | bytes 294920 | tf_op jit(solution)/shard_map/ppermute | solution.py:41
  90.9 30.9 %copy-start.11 = (bf16[256,768]{1,0:T(8,128)(2,1)}, bf16[256,768]{1,0:T(8,128)(2,1)S(1)}, u32[]{:S(2)}) copy-start(bf16[256,768]{1,0:T(8,128)(2,1)S(1)} %multiply_convert_fusion.routed) | copy-start | bytes 1179652
  100.6 16.5 %copy-start.41 = (f32[256]{0:T(256)S(1)}, f32[256]{0:T(256)}, u32[]{:S(2)}) copy-start(f32[256]{0:T(256)} %fusion.21) | copy-start | bytes 3076
  100.6 39.2 %all-to-all-start.2 = ((bf16[8,128,768]{2,1,0:T(8,128)(2,1)}), bf16[8,128,768]{2,1,0:T(8,128)(2,1)S(1)}, u32[]{:S(2)}, u32[]{:S(2)}) async-start(bf16[8,128,768]{2,1,0:T(8,128)(2,1)} %bitcast.180), calls=%async_computation.2 | async-start | bytes 3145728 | tf_op jit(solution)/shard_map/all_to_all | solution.py:611
  118.9 20.9 %collective-permute-start.8 = (bf16[256,768]{1,0:T(8,128)(2,1)S(1)}, bf16[256,768]{1,0:T(8,128)(2,1)}, u32[]{:S(2)}, u32[]{:S(2)}) collective-permute-start(bf16[256,768]{1,0:T(8,128)(2,1)S(1)} %multiply_convert_fusion.routed), channel_id=1, source_target_pairs={{0,2},{1,3},{2,0},{3,1},{4,6},{5,7},{6,4},{7,5},{8,10},{9,11},{10,... | collective-permute-start | bytes 1179656 | tf_op jit(solution)/shard_map/ppermute | solution.py:46
  143.3 33.7 %all-to-all-start.3 = ((bf16[8,128,768]{2,1,0:T(8,128)(2,1)}), bf16[8,128,768]{2,1,0:T(8,128)(2,1)}, u32[]{:S(2)}, u32[]{:S(2)}) async-start(bf16[8,128,768]{2,1,0:T(8,128)(2,1)} %bitcast.181), calls=%async_computation.3 | async-start | bytes 3145728 | tf_op jit(solution)/shard_map/all_to_all | solution.py:611
  179.7 35.1 %all-to-all-start.4 = ((bf16[8,136,768]{2,1,0:T(8,128)(2,1)}), bf16[8,136,768]{2,1,0:T(8,128)(2,1)S(1)}, u32[]{:S(2)}, u32[]{:S(2)}) async-start(bf16[8,136,768]{2,1,0:T(8,128)(2,1)} %get-tuple-element.90), calls=%async_computation.4 | async-start | bytes 3342336 | tf_op jit(solution)/shard_map/all_to_all | solution.py:611
  199.4 43.0 %collective-permute-start.12 = (bf16[1,768,768]{2,1,0:T(8,128)(2,1)}, bf16[1,768,768]{2,1,0:T(8,128)(2,1)}, u32[]{:S(2)}, u32[]{:S(2)}) collective-permute-start(bf16[1,768,768]{2,1,0:T(8,128)(2,1)} %get-tuple-element.100), channel_id=1, source_target_pairs={{0,1},{1,0},{2,3},{3,2},{4,5},{5,4},{6,7},{7,6},{8,9},{9,8},{10,11... | collective-permute-start | bytes 3538952 | tf_op jit(solution)/shard_map/ppermute | solution.py:46
  215.9 16.1 %copy-start.19 = (bf16[4,192,256]{2,1,0:T(8,128)(2,1)S(1)}, bf16[4,192,256]{2,1,0:T(8,128)(2,1)}, u32[]{:S(2)}) copy-start(bf16[4,192,256]{2,1,0:T(8,128)(2,1)} %copy-done.18) | copy-start | bytes 1179652
  224.2 10.9 %collective-permute-start.9 = (bf16[1,192,256]{2,1,0:T(8,128)(2,1)S(1)}, bf16[1,192,256]{2,1,0:T(8,128)(2,1)}, u32[]{:S(2)}, u32[]{:S(2)}) collective-permute-start(bf16[1,192,256]{2,1,0:T(8,128)(2,1)S(1)} %get-tuple-element.153), channel_id=1, source_target_pairs={{0,2},{1,3},{2,0},{3,1},{4,6},{5,7},{6,4},{7,5},{8,10},{9,11},{10,... | collective-permute-start | bytes 294920 | tf_op jit(solution)/shard_map/ppermute | solution.py:41
  226.2 14.9 %collective-permute-start.10 = (bf16[1,192,256]{2,1,0:T(8,128)(2,1)}, bf16[1,192,256]{2,1,0:T(8,128)(2,1)S(1)}, u32[]{:S(2)}, u32[]{:S(2)}) collective-permute-start(bf16[1,192,256]{2,1,0:T(8,128)(2,1)} %get-tuple-element.152), channel_id=1, source_target_pairs={{0,1},{1,2},{2,3},{3,0},{4,5},{5,6},{6,7},{7,4},{8,9},{9,10},{10,1... | collective-permute-start | bytes 294920 | tf_op jit(solution)/shard_map/ppermute | solution.py:41
  227.1 14.7 %collective-permute-start.11 = (bf16[1,192,256]{2,1,0:T(8,128)(2,1)}, bf16[1,192,256]{2,1,0:T(8,128)(2,1)S(1)}, u32[]{:S(2)}, u32[]{:S(2)}) collective-permute-start(bf16[1,192,256]{2,1,0:T(8,128)(2,1)} %get-tuple-element.151), channel_id=1, source_target_pairs={{0,3},{1,0},{2,1},{3,2},{4,7},{5,4},{6,5},{7,6},{8,11},{9,8},{10,9... | collective-permute-start | bytes 294920 | tf_op jit(solution)/shard_map/ppermute | solution.py:41
  234.4 27.2 %collective-permute-start.16 = (bf16[4,96,768]{2,1,0:T(8,128)(2,1)}, bf16[4,96,768]{2,1,0:T(8,128)(2,1)S(1)}, u32[]{:S(2)}, u32[]{:S(2)}) collective-permute-start(bf16[4,96,768]{2,1,0:T(8,128)(2,1)} %dynamic-slice_bitcast_fusion), channel_id=1, source_target_pairs={{0,4},{4,0},{8,12},{12,8},{16,20},{20,16},{24,28},{28,24},{1,5},{5... | collective-permute-start | bytes 1769480 | tf_op jit(solution)/shard_map/ppermute | solution.py:46
  235.1 38.7 %all-to-all-start.5 = ((bf16[8,128,768]{2,1,0:T(8,128)(2,1)}), bf16[8,128,768]{2,1,0:T(8,128)(2,1)}, u32[]{:S(2)}, u32[]{:S(2)}) async-start(bf16[8,128,768]{2,1,0:T(8,128)(2,1)} %bitcast.197), calls=%async_computation.5 | async-start | bytes 3145728 | tf_op jit(solution)/shard_map/all_to_all | solution.py:611
  257.7 22.6 %collective-permute-start.25 = (bf16[1,3,192,256]{3,2,1,0:T(8,128)(2,1)}, bf16[1,3,192,256]{3,2,1,0:T(8,128)(2,1)}, u32[]{:S(2)}, u32[]{:S(2)}) collective-permute-start(bf16[1,3,192,256]{3,2,1,0:T(8,128)(2,1)} %get-tuple-element.145), channel_id=1, source_target_pairs={{0,2},{1,3},{2,0},{3,1},{4,6},{5,7},{6,4},{7,5},{8,10},{9,11},{10,... | collective-permute-start | bytes 884744 | tf_op jit(solution)/shard_map/ppermute | solution.py:41
  257.7 23.6 %collective-permute-start.26 = (bf16[1,3,192,256]{3,2,1,0:T(8,128)(2,1)}, bf16[1,3,192,256]{3,2,1,0:T(8,128)(2,1)}, u32[]{:S(2)}, u32[]{:S(2)}) collective-permute-start(bf16[1,3,192,256]{3,2,1,0:T(8,128)(2,1)} %get-tuple-element.144), channel_id=1, source_target_pairs={{0,1},{1,2},{2,3},{3,0},{4,5},{5,6},{6,7},{7,4},{8,9},{9,10},{10,1... | collective-permute-start | bytes 884744 | tf_op jit(solution)/shard_map/ppermute | solution.py:41
  260.1 31.7 %collective-permute-start.27 = (bf16[1,3,192,256]{3,2,1,0:T(8,128)(2,1)}, bf16[1,3,192,256]{3,2,1,0:T(8,128)(2,1)}, u32[]{:S(2)}, u32[]{:S(2)}) collective-permute-start(bf16[1,3,192,256]{3,2,1,0:T(8,128)(2,1)} %get-tuple-element.143), channel_id=1, source_target_pairs={{0,3},{1,0},{2,1},{3,2},{4,7},{5,4},{6,5},{7,6},{8,11},{9,8},{10,9... | collective-permute-start | bytes 884744 | tf_op jit(solution)/shard_map/ppermute | solution.py:41
  263.8 8.9 %collective-permute-start.17 = (bf16[2,96,768]{2,1,0:T(8,128)(2,1)S(1)}, bf16[2,96,768]{2,1,0:T(8,128)(2,1)S(1)}, u32[]{:S(2)}, u32[]{:S(2)}) collective-permute-start(bf16[2,96,768]{2,1,0:T(8,128)(2,1)S(1)} %fusion.32), channel_id=1, source_target_pairs={{0,16},{4,20},{8,24},{12,28},{16,0},{20,4},{24,8},{28,12},{1,17},{... | collective-permute-start | bytes 884744 | tf_op jit(solution)/shard_map/ppermute | solution.py:46
  275.2 7.1 %collective-permute-start.13 = (bf16[4,80,768]{2,1,0:T(8,128)(2,1)S(1)}, bf16[4,80,768]{2,1,0:T(8,128)(2,1)S(1)}, u32[]{:S(2)}, u32[]{:S(2)}) collective-permute-start(bf16[4,80,768]{2,1,0:T(8,128)(2,1)S(1)} %fusion.29), channel_id=1, source_target_pairs={{0,4},{4,0},{8,12},{12,8},{16,20},{20,16},{24,28},{28,24},{1,5},{5... | collective-permute-start | bytes 1474568 | tf_op jit(solution)/shard_map/ppermute | solution.py:46
  275.3 7.0 %collective-permute-start.18 = (bf16[1,96,768]{2,1,0:T(8,128)(2,1)S(1)}, bf16[1,96,768]{2,1,0:T(8,128)(2,1)S(1)}, u32[]{:S(2)}, u32[]{:S(2)}) collective-permute-start(bf16[1,96,768]{2,1,0:T(8,128)(2,1)S(1)} %dynamic-slice_convert_fusion.2), channel_id=1, source_target_pairs={{0,8},{4,12},{8,0},{12,4},{16,24},{20,28},{24,16},{28,20},{1,9},{5... | collective-permute-start | bytes 442376 | tf_op jit(solution)/shard_map/ppermute | solution.py:46
  282.5 14.8 %collective-permute-start.14 = (bf16[2,80,768]{2,1,0:T(8,128)(2,1)S(1)}, bf16[2,80,768]{2,1,0:T(8,128)(2,1)S(1)}, u32[]{:S(2)}, u32[]{:S(2)}) collective-permute-start(bf16[2,80,768]{2,1,0:T(8,128)(2,1)S(1)} %fusion.35), channel_id=1, source_target_pairs={{0,16},{4,20},{8,24},{12,28},{16,0},{20,4},{24,8},{28,12},{1,17},{... | collective-permute-start | bytes 737288 | tf_op jit(solution)/shard_map/ppermute | solution.py:46
  285.5 20.3 %copy-start.5 = (f32[256,768]{1,0:T(8,128)S(1)}, f32[256,768]{1,0:T(8,128)}, u32[]{:S(2)}) copy-start(f32[256,768]{1,0:T(8,128)} %copy-done.4) | copy-start | bytes 2359300
  285.5 20.3 %copy-start.40 = (s32[256,8]{0,1:T(8,128)S(1)}, s32[256,8]{0,1:T(8,128)}, u32[]{:S(2)}) copy-start(s32[256,8]{0,1:T(8,128)} %copy-done.39) | copy-start | bytes 24580
  285.5 11.1 %collective-permute-start.19 = (bf16[1,24,768]{2,1,0:T(8,128)(2,1)S(1)}, bf16[1,24,768]{2,1,0:T(8,128)(2,1)S(1)}, u32[]{:S(2)}, u32[]{:S(2)}) collective-permute-start(bf16[1,24,768]{2,1,0:T(8,128)(2,1)S(1)} %get-tuple-element.161), channel_id=1, source_target_pairs={{0,2},{1,3},{2,0},{3,1},{4,6},{5,7},{6,4},{7,5},{8,10},{9,11},{10,... | collective-permute-start | bytes 110600 | tf_op jit(solution)/shard_map/ppermute | solution.py:41
  292.8 7.5 %collective-permute-start.20 = (bf16[1,24,768]{2,1,0:T(8,128)(2,1)S(1)}, bf16[1,24,768]{2,1,0:T(8,128)(2,1)S(1)}, u32[]{:S(2)}, u32[]{:S(2)}) collective-permute-start(bf16[1,24,768]{2,1,0:T(8,128)(2,1)S(1)} %get-tuple-element.160), channel_id=1, source_target_pairs={{0,1},{1,2},{2,3},{3,0},{4,5},{5,6},{6,7},{7,4},{8,9},{9,10},{10,1... | collective-permute-start | bytes 110600 | tf_op jit(solution)/shard_map/ppermute | solution.py:41
  292.8 8.0 %collective-permute-start.21 = (bf16[1,24,768]{2,1,0:T(8,128)(2,1)S(1)}, bf16[1,24,768]{2,1,0:T(8,128)(2,1)S(1)}, u32[]{:S(2)}, u32[]{:S(2)}) collective-permute-start(bf16[1,24,768]{2,1,0:T(8,128)(2,1)S(1)} %get-tuple-element.159), channel_id=1, source_target_pairs={{0,3},{1,0},{2,1},{3,2},{4,7},{5,4},{6,5},{7,6},{8,11},{9,8},{10,9... | collective-permute-start | bytes 110600 | tf_op jit(solution)/shard_map/ppermute | solution.py:41
  298.8 5.2 %collective-permute-start.15 = (bf16[1,80,768]{2,1,0:T(8,128)(2,1)}, bf16[1,80,768]{2,1,0:T(8,128)(2,1)}, u32[]{:S(2)}, u32[]{:S(2)}) collective-permute-start(bf16[1,80,768]{2,1,0:T(8,128)(2,1)} %dynamic-slice_convert_fusion.3), channel_id=1, source_target_pairs={{0,8},{4,12},{8,0},{12,4},{16,24},{20,28},{24,16},{28,20},{1,9},{5... | collective-permute-start | bytes 368648 | tf_op jit(solution)/shard_map/ppermute | solution.py:46
  305.8 8.3 %collective-permute-start.22 = (bf16[1,104,768]{2,1,0:T(8,128)(2,1)S(1)}, bf16[1,104,768]{2,1,0:T(8,128)(2,1)S(1)}, u32[]{:S(2)}, u32[]{:S(2)}) collective-permute-start(bf16[1,104,768]{2,1,0:T(8,128)(2,1)S(1)} %maximum_bitcast_fusion.2), channel_id=1, source_target_pairs={{0,1},{1,2},{2,3},{3,0},{4,5},{5,6},{6,7},{7,4},{8,9},{9,10},{10,1... | collective-permute-start | bytes 479240 | tf_op jit(solution)/shard_map/ppermute | solution.py:41
  310.2 6.6 %collective-permute-start.23 = (bf16[1,104,768]{2,1,0:T(8,128)(2,1)S(1)}, bf16[1,104,768]{2,1,0:T(8,128)(2,1)S(1)}, u32[]{:S(2)}, u32[]{:S(2)}) collective-permute-start(bf16[1,104,768]{2,1,0:T(8,128)(2,1)S(1)} %maximum_bitcast_fusion.2), channel_id=1, source_target_pairs={{0,3},{1,0},{2,1},{3,2},{4,7},{5,4},{6,5},{7,6},{8,11},{9,8},{10,9... | collective-permute-start | bytes 479240 | tf_op jit(solution)/shard_map/ppermute | solution.py:41
  314.1 8.7 %collective-permute-start.24 = (bf16[1,104,768]{2,1,0:T(8,128)(2,1)S(1)}, bf16[1,104,768]{2,1,0:T(8,128)(2,1)S(1)}, u32[]{:S(2)}, u32[]{:S(2)}) collective-permute-start(bf16[1,104,768]{2,1,0:T(8,128)(2,1)S(1)} %collective-permute-done.22), channel_id=1, source_target_pairs={{0,1},{1,2},{2,3},{3,0},{4,5},{5,6},{6,7},{7,4},{8,9},{9,10},{10,1... | collective-permute-start | bytes 479240 | tf_op jit(solution)/shard_map/ppermute | solution.py:41
  322.9 24.5 %collective-permute-start.32 = (bf16[1,768,768]{2,1,0:T(8,128)(2,1)S(1)}, bf16[1,768,768]{2,1,0:T(8,128)(2,1)S(1)}, u32[]{:S(2)}, u32[]{:S(2)}) collective-permute-start(bf16[1,768,768]{2,1,0:T(8,128)(2,1)S(1)} %copy-done.43), channel_id=1, source_target_pairs={{0,1},{1,0},{2,3},{3,2},{4,5},{5,4},{6,7},{7,6},{8,9},{9,8},{10,11... | collective-permute-start | bytes 3538952 | tf_op jit(solution)/shard_map/ppermute | solution.py:46
  323.6 8.5 %collective-permute-start.29 = (bf16[4,104,384]{2,1,0:T(8,128)(2,1)S(1)}, bf16[4,104,384]{2,1,0:T(8,128)(2,1)S(1)}, u32[]{:S(2)}, u32[]{:S(2)}) collective-permute-start(bf16[4,104,384]{2,1,0:T(8,128)(2,1)S(1)} %get-tuple-element.149), channel_id=1, source_target_pairs={{0,16},{4,20},{8,24},{12,28},{16,0},{20,4},{24,8},{28,12},{1,17},{... | collective-permute-start | bytes 958472 | tf_op jit(solution)/shard_map/ppermute | solution.py:46
  324.0 8.1 %collective-permute-start.28 = (bf16[4,104,384]{2,1,0:T(8,128)(2,1)S(1)}, bf16[4,104,384]{2,1,0:T(8,128)(2,1)S(1)}, u32[]{:S(2)}, u32[]{:S(2)}) collective-permute-start(bf16[4,104,384]{2,1,0:T(8,128)(2,1)S(1)} %get-tuple-element.150), channel_id=1, source_target_pairs={{0,8},{4,12},{8,0},{12,4},{16,24},{20,28},{24,16},{28,20},{1,9},{5... | collective-permute-start | bytes 958472 | tf_op jit(solution)/shard_map/ppermute | solution.py:46
  332.3 12.1 %collective-permute-start.30 = (bf16[2,4,104,384]{3,2,1,0:T(8,128)(2,1)S(1)}, bf16[2,4,104,384]{3,2,1,0:T(8,128)(2,1)S(1)}, u32[]{:S(2)}, u32[]{:S(2)}) collective-permute-start(bf16[2,4,104,384]{3,2,1,0:T(8,128)(2,1)S(1)} %pad_maximum_fusion.2), channel_id=1, source_target_pairs={{0,16},{4,20},{8,24},{12,28},{16,0},{20,4},{24,8},{28,12},{1,17},{... | collective-permute-start | bytes 1916936 | tf_op jit(solution)/shard_map/ppermute | solution.py:46
  333.8 11.5 %collective-permute-start.31 = (bf16[2,4,104,384]{3,2,1,0:T(8,128)(2,1)S(1)}, bf16[2,4,104,384]{3,2,1,0:T(8,128)(2,1)S(1)}, u32[]{:S(2)}, u32[]{:S(2)}) collective-permute-start(bf16[2,4,104,384]{3,2,1,0:T(8,128)(2,1)S(1)} %pad_maximum_fusion.3), channel_id=1, source_target_pairs={{0,8},{4,12},{8,0},{12,4},{16,24},{20,28},{24,16},{28,20},{1,9},{5... | collective-permute-start | bytes 1916936 | tf_op jit(solution)/shard_map/ppermute | solution.py:46
  347.4 4.8 %collective-permute-start.33 = (bf16[2,2,2,4,104,384]{5,4,3,2,1,0:T(8,128)(2,1)S(1)}, bf16[2,2,2,4,104,384]{5,4,3,2,1,0:T(8,128)(2,1)S(1)}, u32[]{:S(2)}, u32[]{:S(2)}) collective-permute-start(bf16[2,2,2,4,104,384]{5,4,3,2,1,0:T(8,128)(2,1)S(1)} %pad_maximum_fusion.near), channel_id=1, source_target_pairs={{0,4},{4,0},{8,12},{12,8},{16,20},{20,16},{24,28},{28,24},{1,5},{5... | collective-permute-start | bytes 7667720 | tf_op jit(solution)/shard_map/ppermute | solution.py:46
  (38 other events, 197.3 us)
